TPU v7x, 32 devices: a whole 2x2x4 slice. The times are simulated.
32 devices in a mesh: row: 16 (over z, y, core), col: 2 (over x).
Axes of the slice: x: 2, y: 2, z: 4, core: 2. Of those that a mesh axis runs over, the one named last changes fastest.
Arguments:
- blocks: bfloat16 [160, 72, 128, 128], P('row', 'col')
- slot_cols: int32 [160, 72], P('row', 'col'), may hold values from 0 to 79, as said below
- counts: int32 [160, 2], P('row', 'col'), may hold values from 2 to 36, as said below
- demand: bfloat16 [20480, 128], P('col'), may hold values from 0.1 to 10
- value_added: float32 [20480], P('col'), may hold values from 0.5 to 5
Outputs:
- propagated: bfloat16 [20480, 128], P('row')
Inputs may be any that keep to these rules, and one draw needn't show every extreme that they name: `counts`: some block row has all 36 slots live in every column group; live slots come first in each group. `slot_cols`: within one block row and column group the 36 slots name distinct column blocks.
All inputs are finite; a program needn't handle non-finite values.
Results may differ from a plain program's by a relative error of at most 0.0042.
Values may be sent and summed in bfloat16 or wider, within the bound.
No kernel may reach another device: no remote copies, remote signals or barrier semaphores. Data moves between devices by JAX's collectives and lax.ppermute only.
A program may use at most 128 MiB of HBM per device.

v0:
```python
import functools

import jax
import jax.numpy as jnp
from jax import lax
from jax.experimental import pallas as pl
from jax.experimental.pallas import tpu as pltpu
from jax.sharding import PartitionSpec as P

VMEM_LIMIT = 12 * 1024 * 1024


def slot_ranges(slots):
    first = min(12, slots)
    return [range(first)] + ([range(first, slots)] if slots > first else [])


def sums_kernel(cols_hbm, counts_hbm, blocks_ref, sums_ref, held_ref, acc_ref, cols_ref, counts_ref, list_sems, sems):
    rows, slots, size, _ = blocks_ref.shape
    groups = acc_ref.shape[0] - 1
    first, *others = slot_ranges(slots)
    others = [range(start, min(start + 12, slots)) for other in others for start in range(other.start, slots, 12)]

    def fetch(b, part):
        span = pl.ds(part.start, len(part))
        return pltpu.make_async_copy(blocks_ref.at[b, span], held_ref.at[b, span], sems.at[b, part.start // 12])

    counts_copy = pltpu.make_async_copy(counts_hbm, counts_ref, list_sems.at[0])
    cols_copy = pltpu.make_async_copy(cols_hbm, cols_ref, list_sems.at[1])
    counts_copy.start()
    cols_copy.start()
    for b in range(rows):
        fetch(b, first).start()
    acc_ref[...] = jnp.zeros_like(acc_ref)
    counts_copy.wait()
    cols_copy.wait()
    def for_heavy_rows(action):
        def one_row(b, carry):
            @pl.when(counts_ref[b] > len(first))
            def _():
                for part in others:
                    action(b, part)

            return carry

        if others:
            lax.fori_loop(0, rows, one_row, 0)

    def add(b, part):
        fetch(b, part).wait()
        for slot in part:
            col = jnp.where(slot < counts_ref[b], cols_ref[b, slot], groups)
            block = held_ref[b, slot].astype(jnp.float32)
            acc_ref[col] += jnp.sum(block.reshape(size // 8, 8, size), axis=0)

    def add_first(b, carry):
        add(b, first)
        return carry

    for_heavy_rows(lambda b, part: fetch(b, part).start())
    lax.fori_loop(0, rows, add_first, 0)
    for_heavy_rows(add)
    sums_ref[...] = jnp.sum(acc_ref[:groups], axis=1)


def multiply_rows(rows, counts_ref, slots, start, gather, acc_ref):
    first, *others = slot_ranges(slots)

    def product(row, part):
        left, right = zip(*[gather(row, slot) for slot in part])
        return jnp.dot(jnp.concatenate(left, axis=1), jnp.concatenate(right, axis=0), preferred_element_type=jnp.float32)

    for b, row in enumerate(rows):
        acc_ref[b] = start(b) + product(row, first)
    def one_row(b, carry):
        row = rows[0] + b
        for part in others:

            @pl.when(counts_ref[row] > part.start)
            def _():
                acc_ref[b] += product(row, part)

        return carry

    if others:
        lax.fori_loop(0, len(rows), one_row, 0)


def scaled_block(row, slot, cols_ref, counts_ref, inverse_ref, blocks_ref):
    size = blocks_ref.shape[2]
    scale = jnp.where(slot < counts_ref[row], inverse_ref[pl.ds(cols_ref[row, slot], 1), :], 0.0)
    scale = jnp.broadcast_to(scale, (16, size)).astype(jnp.bfloat16)
    return (blocks_ref[row, slot].reshape(size // 16, 16, size) * scale).reshape(size, size)


def first_row(sending, count):
    if sending is None:
        return 0
    side = lax.axis_index("col")
    return (1 - side if sending else side) * count


def first_kernel(sending, cols_ref, counts_ref, sums_ref, added_ref, demand_ref, blocks_ref, *rest):
    inverse_ref, acc_ref = rest[-2:]
    if sending:
        out_ref, coef_ref = rest[-3], None
    else:
        out_ref, coef_ref = rest[-4:-2]
    slots = blocks_ref.shape[1]
    count = out_ref.shape[0]
    inverse_ref[...] = 1.0 / (sums_ref[...] + added_ref[...])

    def gather(row, slot):
        coef = scaled_block(row, slot, cols_ref, counts_ref, inverse_ref, blocks_ref)
        if coef_ref is not None:
            coef_ref[row, slot] = coef
        return coef, demand_ref[cols_ref[row, slot]]

    rows = [first_row(sending, count) + b for b in range(count)]
    multiply_rows(rows, counts_ref, slots, lambda b: 0.0, gather, acc_ref)
    out_ref[...] = acc_ref[...].astype(out_ref.dtype)


def scale_kernel(count, cols_ref, counts_ref, sums_ref, added_ref, blocks_ref, coef_ref, token_ref, inverse_ref):
    first, *others = slot_ranges(blocks_ref.shape[1])
    inverse_ref[...] = 1.0 / (sums_ref[...] + added_ref[...])
    token_ref[...] = inverse_ref[:8]

    def scale(row, part):
        for slot in part:
            coef_ref[row, slot] = scaled_block(row, slot, cols_ref, counts_ref, inverse_ref, blocks_ref)

    rows = [first_row(True, count) + b for b in range(count)]
    for row in rows:
        scale(row, first)
    def one_row(b, carry):
        row = rows[0] + b
        for part in others:

            @pl.when(counts_ref[row] > part.start)
            def _():
                scale(row, part)

        return carry

    if others:
        lax.fori_loop(0, len(rows), one_row, 0)


def fetch_kernel(demand_hbm, _, demand_ref, sem):
    copy = pltpu.make_async_copy(demand_hbm, demand_ref, sem)
    copy.start()
    copy.wait()


def second_rows(first_row, place, cols_ref, counts_ref, coef_ref, source_ref, start, out_ref, acc_ref):
    slots = coef_ref.shape[1]

    def gather(row, slot):
        return coef_ref[row, slot], source_ref[place(cols_ref[row, slot])]

    rows = [first_row + b for b in range(out_ref.shape[0])]
    multiply_rows(rows, counts_ref, slots, start, gather, acc_ref)
    out_ref[...] = acc_ref[...].astype(out_ref.dtype)


def exact_scale(count, part):
    scale = -(-(1 << 16) // part)
    assert all((i * scale) >> 16 == i // part for i in range(count))
    return scale


HOME = ((0, 0, 0), (0, 1, 0), (1, 0, 0), (1, 1, 0))
AWAY = ((0, 0, 1), (0, 1, 1), (1, 0, 1), (1, 1, 1))


def collect(array, places, core, source_ref):
    part = array.shape[0] // len(places)
    for i, (z, y, away) in enumerate(places):
        at = ((z * 4 + y * 2 + core) * 2 + away) * part
        source_ref[at : at + part] = array[i * part : (i + 1) * part]


def collect_kernel(home_ref, away_ref, home_core_ref, source_ref):
    collect(home_ref, HOME, 0, source_ref)
    collect(away_ref, AWAY, 0, source_ref)
    collect(home_core_ref, HOME, 1, source_ref)


def second_part_kernel(which, cols_ref, counts_ref, coef_ref, own_ref, *rest):
    part = own_ref.shape[0]
    if which == 0:
        _, away_core_ref, out_ref, source_ref, acc_ref = rest
        collect(away_core_ref, AWAY, 1, source_ref)
    else:
        source_ref, out_ref, acc_ref = rest
    side = lax.axis_index("col")
    near = lax.rem(lax.axis_index("row"), 8) * 2 + side
    scale = exact_scale(source_ref.shape[0], part)

    def place(col):
        piece = lax.shift_right_logical(col * scale, 16)
        return col + part * ((piece ^ near) - piece)

    def start(b):
        return jnp.where(side == which, own_ref[b].astype(jnp.float32), 0.0)

    second_rows(which * part, place, cols_ref, counts_ref, coef_ref, source_ref, start, out_ref, acc_ref)


def second_kernel(cols_ref, counts_ref, coef_ref, own_ref, source_ref, out_ref, acc_ref):
    first = lax.axis_index("col") == 0

    def start(b):
        return jnp.where(first, own_ref[b].astype(jnp.float32), 0.0)

    second_rows(0, lambda col: col, cols_ref, counts_ref, coef_ref, source_ref, start, out_ref, acc_ref)


def choose_kernel(own_ref, crossed_ref, _, home_ref, away_ref):
    owner = lax.div(lax.axis_index("row"), 8) == lax.axis_index("col")

    @pl.when(owner)
    def _():
        home_ref[...] = own_ref[...]
        away_ref[...] = crossed_ref[...]

    @pl.when(jnp.logical_not(owner))
    def _():
        home_ref[...] = crossed_ref[...]
        away_ref[...] = own_ref[...]


def join_kernel(*refs):
    pieces, joined_ref = refs[:-1], refs[-1]
    part = pieces[0].shape[0]
    for i, piece in enumerate(pieces):
        joined_ref[i * part : (i + 1) * part] = piece[...]


def result_kernel(first_row, mine_ref, other_ref, *rest):
    out_ref, sum_ref, sem = rest[-3:]
    sum_ref[...] = (mine_ref[...].astype(jnp.float32) + other_ref[...].astype(jnp.float32)).astype(sum_ref.dtype)
    copy = pltpu.make_async_copy(sum_ref, out_ref.at[pl.ds(first_row, sum_ref.shape[0])], sem)
    copy.start()
    copy.wait()


SMEM = pl.BlockSpec(memory_space=pltpu.SMEM)
VMEM = pl.BlockSpec(memory_space=pltpu.VMEM)
PARAMS = pltpu.CompilerParams(vmem_limit_bytes=VMEM_LIMIT)


def cost(flops, bytes_accessed):
    return pl.CostEstimate(flops=flops, bytes_accessed=bytes_accessed, transcendentals=0)


def in_vmem(array):
    return pltpu.with_memory_space_constraint(array, pltpu.VMEM)


def body(n_row, n_col, blocks, slot_cols, counts, demand, value_added):
    rows, slots, size, _ = blocks.shape
    width = demand.shape[1]
    groups = demand.shape[0] // size
    group_devices = n_row // n_col
    paired = n_col == 2 and n_row == 16 and rows % 2 == 0
    half = rows // 2
    counts = counts.reshape(rows)

    sums, held = pl.pallas_call(
        sums_kernel,
        name="column_sums",
        out_shape=(
            jax.ShapeDtypeStruct((groups, size), jnp.float32),
            pltpu.VMEM(blocks.shape, blocks.dtype),
        ),
        in_specs=[pl.BlockSpec(memory_space=pltpu.HBM)] * 3,
        out_specs=(VMEM, VMEM),
        scratch_shapes=[
            pltpu.VMEM((groups + 1, 8, size), jnp.float32),
            pltpu.SMEM(slot_cols.shape, jnp.int32),
            pltpu.SMEM(counts.shape, jnp.int32),
            pltpu.SemaphoreType.DMA((2,)),
            pltpu.SemaphoreType.DMA((rows, -(-slots // 12))),
        ],
        compiler_params=PARAMS,
        cost_estimate=cost(0, 4 * rows * size * size * slots),
    )(*[pltpu.with_memory_space_constraint(array, pltpu.HBM) for array in (slot_cols, counts, blocks)])

    def flip(array, mask):
        return lax.ppermute(array, "row", [(i, i ^ mask) for i in range(n_row)])

    def swap(array):
        return lax.ppermute(array, "col", [(0, 1), (1, 0)])

    if paired:
        for masks in ((1, 2, 3), (4, 8, 12)):
            sums = sums.astype(jnp.bfloat16)
            parts = [sums] + [flip(sums, m) for m in masks]
            if masks[0] == 4:
                demand = pl.pallas_call(
                    fetch_kernel,
                    name="own_demand",
                    out_shape=pltpu.VMEM(demand.shape, demand.dtype),
                    in_specs=[pl.BlockSpec(memory_space=pltpu.HBM), pl.BlockSpec(memory_space=pl.ANY)],
                    out_specs=VMEM,
                    scratch_shapes=[pltpu.SemaphoreType.DMA],
                    compiler_params=PARAMS,
                    cost_estimate=cost(0, 3 * demand.size * 2),
                )(pltpu.with_memory_space_constraint(demand, pltpu.HBM), sums)
            sums = functools.reduce(jnp.add, [part.astype(jnp.float32) for part in parts])
    else:
        sums = lax.psum(sums, "row")

    def layer_cost(count):
        return cost(2 * count * slots * size * size * width, count * slots * size * size * 2)

    def first_layer(sending, count, dtype, held, earlier=()):
        out = jax.ShapeDtypeStruct((count, size, width), dtype)
        return pl.pallas_call(
            functools.partial(first_kernel, sending),
            name="first_layer",
            out_shape=out if sending else (out, pltpu.VMEM(blocks.shape, blocks.dtype)),
            in_specs=[SMEM, SMEM, VMEM, VMEM, VMEM, VMEM] + [pl.BlockSpec(memory_space=pl.ANY)] * len(earlier),
            out_specs=VMEM if sending else (VMEM, VMEM),
            scratch_shapes=[
                pltpu.VMEM((groups, size), jnp.float32),
                pltpu.VMEM((count, size, width), jnp.float32),
            ],
            input_output_aliases={} if sending else {5: 1},
            compiler_params=PARAMS,
            cost_estimate=layer_cost(count),
        )(
            slot_cols,
            counts,
            sums,
            value_added.reshape(groups, size),
            demand.reshape(groups, size, width),
            in_vmem(held),
            *earlier,
        )

    def second_call(kernel, count, coefs, own, sources, keep_sources):
        dtype = jnp.bfloat16 if paired else jnp.float32
        out = jax.ShapeDtypeStruct((count, size, width), dtype)
        return pl.pallas_call(
            kernel,
            name="second_layer",
            out_shape=(out, pltpu.VMEM((groups, size, width), jnp.bfloat16)) if keep_sources else out,
            input_output_aliases={4: 1} if keep_sources else {},
            in_specs=[SMEM, SMEM] + [VMEM] * (2 + len(sources)),
            out_specs=(VMEM, VMEM) if keep_sources else VMEM,
            scratch_shapes=[pltpu.VMEM((count, size, width), jnp.float32)],
            compiler_params=PARAMS,
            cost_estimate=layer_cost(count),
        )(slot_cols, counts, in_vmem(coefs), own, *sources)

    if not paired:
        group = lax.axis_index("col")
        partial, coefs = first_layer(None, rows, jnp.float32, held)
        layer_one = lax.psum(partial, "col").astype(jnp.bfloat16)
        gathered = lax.all_gather(layer_one, "row", axis=0, tiled=True)
        source = lax.dynamic_slice_in_dim(gathered, group * groups, groups, 0)
        partial = second_call(second_kernel, rows, coefs, layer_one, [source], False)
        return lax.psum(partial, "col").astype(jnp.bfloat16).reshape(rows * size, width)

    sent = first_layer(True, half, jnp.bfloat16, held)
    arrived = swap(sent)
    kept, coefs = first_layer(False, half, jnp.float32, held, [sent])
    coefs, token = pl.pallas_call(
        functools.partial(scale_kernel, half),
        name="own_coefficients",
        out_shape=(pltpu.VMEM(blocks.shape, blocks.dtype), jax.ShapeDtypeStruct((8, size), jnp.float32)),
        in_specs=[SMEM, SMEM, VMEM, VMEM, VMEM],
        out_specs=(VMEM, VMEM),
        scratch_shapes=[pltpu.VMEM((groups, size), jnp.float32)],
        input_output_aliases={4: 0},
        compiler_params=PARAMS,
        cost_estimate=layer_cost(half),
    )(slot_cols, counts, sums, value_added.reshape(groups, size), in_vmem(coefs))
    own = (kept + arrived.astype(jnp.float32)).astype(jnp.bfloat16)

    piece = jax.ShapeDtypeStruct(own.shape, own.dtype)
    home, away = pl.pallas_call(
        choose_kernel,
        name="home_and_away",
        out_shape=(piece, piece),
        in_specs=[VMEM] * 3,
        out_specs=(VMEM, VMEM),
        compiler_params=PARAMS,
    )(own, flip(own, group_devices), token)

    def join(pieces):
        return pl.pallas_call(
            join_kernel,
            name="own_joined",
            out_shape=jax.ShapeDtypeStruct((len(pieces) * half, size, width), own.dtype),
            in_specs=[VMEM] * len(pieces),
            out_specs=VMEM,
            compiler_params=PARAMS,
        )(*pieces)

    away = swap(away)
    home, away = [join([part] + [flip(part, mask) for mask in (2, 4, 6)]) for part in (home, away)]
    home_core, away_core = flip(home, 1), flip(away, 1)
    source = pl.pallas_call(
        collect_kernel,
        name="own_collected",
        out_shape=pltpu.VMEM((groups, size, width), jnp.bfloat16),
        in_specs=[VMEM] * 3,
        out_specs=VMEM,
        compiler_params=PARAMS,
        cost_estimate=cost(0, 2 * groups * size * width * 2),
    )(home, away, home_core)

    part_a, source = second_call(
        functools.partial(second_part_kernel, 0), half, coefs, own, [in_vmem(source), away_core], True
    )
    other_a = swap(part_a)
    part_b = second_call(functools.partial(second_part_kernel, 1), half, coefs, own, [in_vmem(source)], False)
    other_b = swap(part_b)

    def result(first_row, inputs):
        return pl.pallas_call(
            functools.partial(result_kernel, first_row),
            name="result",
            out_shape=jax.ShapeDtypeStruct((rows, size, width), jnp.bfloat16),
            in_specs=[VMEM, VMEM] + [pl.BlockSpec(memory_space=pltpu.HBM)] * (len(inputs) - 2),
            out_specs=pl.BlockSpec(memory_space=pltpu.HBM),
            scratch_shapes=[pltpu.VMEM(piece.shape, piece.dtype), pltpu.SemaphoreType.DMA],
            input_output_aliases={2: 0} if len(inputs) > 2 else {},
            compiler_params=PARAMS,
        )(*inputs)

    out = result(0, [part_a, other_a])
    return result(half, [part_b, other_b, out]).reshape(rows * size, width)


def solution(mesh):
    return jax.shard_map(
        functools.partial(body, mesh.shape["row"], mesh.shape["col"]),
        mesh=mesh,
        in_specs=(
            P("row", "col", None, None),
            P("row", "col"),
            P("row", "col"),
            P("col", None),
            P("col"),
        ),
        out_specs=P("row", None),
        check_vma=False,
    )
```

profile of v0, /device:TPU:0, one launch (start us, length us, event | category | flops | bytes accessed | tf_op | source)
XLA Modules:
  0.0 66.1 jit_solution(7340157003275298729)
XLA Ops:
  0.0 0.0 copy-start.1
  0.0 0.0 copy-start.2
  0.0 0.0 copy-start
  0.0 3.0 %column_sums.1 = (f32[80,128]{1,0:T(8,128)S(1)}, bf16[10,36,128,128]{3,2,1,0:T(8,128)(2,1)S(1)}) custom-call(s32[10,36]{1,0:T(8,128)} %cols_ref.9, s32[10]{0:T(128)} %bitcast.9, bf16[10,36,128,128]{3,2,1,0:T(8,128)(2,1)} %blocks_ref.1), custom_call_target="tpu_custom_call" | custom-call | bytes 23592960 | tf_op jit(solution)/shard_map/column_sums/pallas_call | solution.py:271
  3.0 2.7 %collective-permute-start.1 = (bf16[80,128]{1,0:T(8,128)(2,1)S(1)}, bf16[80,128]{1,0:T(8,128)(2,1)S(1)}, u32[]{:S(2)}, u32[]{:S(2)}) collective-permute-start(bf16[80,128]{1,0:T(8,128)(2,1)S(1)} %convert_element_type.36), channel_id=1, source_target_pairs={{0,4},{2,6},{4,0},{6,2},{8,12},{10,14},{12,8},{14,10},{16,20},{18,... | collective-permute-start | bytes 61448 | tf_op jit(solution)/shard_map/ppermute | solution.py:292
  5.7 0.1 collective-permute-start
  5.9 0.0 collective-permute-start.2
  5.9 1.6 %collective-permute-done.1 = bf16[80,128]{1,0:T(8,128)(2,1)S(1)} collective-permute-done((bf16[80,128]{1,0:T(8,128)(2,1)S(1)}, bf16[80,128]{1,0:T(8,128)(2,1)S(1)}, u32[]{:S(2)}, u32[]{:S(2)}) %collective-permute-start.1) | collective-permute-done | bytes 20512 | tf_op jit(solution)/shard_map/ppermute | solution.py:292
  7.5 0.0 collective-permute-done
  7.5 1.6 %collective-permute-done.2 = bf16[80,128]{1,0:T(8,128)(2,1)S(1)} collective-permute-done((bf16[80,128]{1,0:T(8,128)(2,1)S(1)}, bf16[80,128]{1,0:T(8,128)(2,1)S(1)}, u32[]{:S(2)}, u32[]{:S(2)}) %collective-permute-start.2) | collective-permute-done | bytes 20512 | tf_op jit(solution)/shard_map/ppermute | solution.py:292
  9.1 4.5 %collective-permute-start.5 = (bf16[80,128]{1,0:T(8,128)(2,1)S(1)}, bf16[80,128]{1,0:T(8,128)(2,1)S(1)}, u32[]{:S(2)}, u32[]{:S(2)}) collective-permute-start(bf16[80,128]{1,0:T(8,128)(2,1)S(1)} %add_convert_fusion.1._), channel_id=1, source_target_pairs={{0,24},{2,26},{4,28},{6,30},{8,16},{10,18},{12,20},{14,22},{16,8},... | collective-permute-start | bytes 61448 | tf_op jit(solution)/shard_map/ppermute | solution.py:292
  13.6 0.0 collective-permute-start.4
  13.6 0.6 collective-permute-start.3
  14.3 1.7 %own_demand.1 = bf16[10240,128]{1,0:T(8,128)(2,1)S(1)} custom-call(bf16[10240,128]{1,0:T(8,128)(2,1)} %demand_hbm.1, bf16[80,128]{1,0:T(8,128)(2,1)S(1)} %add_convert_fusion.1._), custom_call_target="tpu_custom_call" | custom-call | bytes 7864320 | tf_op jit(solution)/shard_map/own_demand/pallas_call | solution.py:302
  16.0 0.0 collective-permute-done.5
  16.0 2.3 %collective-permute-done.4 = bf16[80,128]{1,0:T(8,128)(2,1)S(1)} collective-permute-done((bf16[80,128]{1,0:T(8,128)(2,1)S(1)}, bf16[80,128]{1,0:T(8,128)(2,1)S(1)}, u32[]{:S(2)}, u32[]{:S(2)}) %collective-permute-start.4) | collective-permute-done | bytes 20512 | tf_op jit(solution)/shard_map/ppermute | solution.py:292
  18.3 0.0 collective-permute-done.3
  18.3 0.0 copy-done.1
  18.3 0.0 copy-done.2
  18.4 0.0 copy-done
  18.4 1.9 %first_layer.2.rest_0_ = bf16[5,128,128]{2,1,0:T(8,128)(2,1)S(1)} custom-call(s32[10,36]{1,0:T(8,128)S(1)} %copy-done.1, s32[10]{0:T(128)S(1)} %bitcast.10, f32[80,128]{1,0:T(8,128)S(1)} %convert_add_fusion.sums_ref, f32[80,128]{1,0:T(8,128)S(1)} %bitcast.6, bf16[80,128,128]{2,1,0:T(8,128)(2,1)S(1)} %bitcast.4, ...), custom_call_target="tpu_custom_call" | custom-call | flops 754974720 | bytes 5898240 | tf_op jit(solution)/shard_map/first_layer/pallas_call | solution.py:321
  20.2 1.2 %collective-permute-start.6 = (bf16[5,128,128]{2,1,0:T(8,128)(2,1)S(1)}, bf16[5,128,128]{2,1,0:T(8,128)(2,1)S(1)}, u32[]{:S(2)}, u32[]{:S(2)}) collective-permute-start(bf16[5,128,128]{2,1,0:T(8,128)(2,1)S(1)} %first_layer.2.rest_0_), channel_id=1, source_target_pairs={{0,1},{1,0},{2,3},{3,2},{4,5},{5,4},{6,7},{7,6},{8,9},{9,8},{10,11... | collective-permute-start | bytes 491528 | tf_op jit(solution)/shard_map/ppermute | solution.py:295
  21.4 2.0 %first_layer.3 = (f32[5,128,128]{2,1,0:T(8,128)S(1)}, bf16[10,36,128,128]{3,2,1,0:T(8,128)(2,1)S(1)}) custom-call(s32[10,36]{1,0:T(8,128)S(1)} %copy-done.1, s32[10]{0:T(128)S(1)} %bitcast.11, f32[80,128]{1,0:T(8,128)S(1)} %convert_add_fusion.sums_ref, f32[80,128]{1,0:T(8,128)S(1)} %bitcast.7, ...), custom_call_target="tpu_custom_call", output_to_operand_aliasing={{1}: (5, {})} | custom-call | flops 754974720 | bytes 5898240 | tf_op jit(solution)/shard_map/first_layer/pallas_call | solution.py:321
  23.4 2.2 %collective-permute-done.6 = bf16[5,128,128]{2,1,0:T(8,128)(2,1)S(1)} collective-permute-done((bf16[5,128,128]{2,1,0:T(8,128)(2,1)S(1)}, bf16[5,128,128]{2,1,0:T(8,128)(2,1)S(1)}, u32[]{:S(2)}, u32[]{:S(2)}) %collective-permute-start.6) | collective-permute-done | bytes 163872 | tf_op jit(solution)/shard_map/ppermute | solution.py:295
  25.7 2.8 %collective-permute-start.7 = (bf16[5,128,128]{2,1,0:T(8,128)(2,1)S(1)}, bf16[5,128,128]{2,1,0:T(8,128)(2,1)S(1)}, u32[]{:S(2)}, u32[]{:S(2)}) collective-permute-start(bf16[5,128,128]{2,1,0:T(8,128)(2,1)S(1)} %add_convert_fusion.own_ref), channel_id=1, source_target_pairs={{0,16},{2,18},{4,20},{6,22},{8,24},{10,26},{12,28},{14,30},{16,0},... | collective-permute-start | bytes 491528 | tf_op jit(solution)/shard_map/ppermute | solution.py:292
  28.5 1.4 %own_coefficients.1 = (bf16[10,36,128,128]{3,2,1,0:T(8,128)(2,1)S(1)}, f32[8,128]{1,0:T(8,128)S(1)}) custom-call(s32[10,36]{1,0:T(8,128)S(1)} %copy-done.1, s32[10]{0:T(128)S(1)} %bitcast.12, f32[80,128]{1,0:T(8,128)S(1)} %convert_add_fusion.sums_ref, f32[80,128]{1,0:T(8,128)S(1)} %bitcast.8, ...), custom_call_target="tpu_custom_call", output_to_operand_aliasing={{0}: (4, {})} | custom-call | flops 754974720 | bytes 5898240 | tf_op jit(solution)/shard_map/own_coefficients/pallas_call | solution.py:371
  29.9 4.3 %collective-permute-done.7.crossed_ref = bf16[5,128,128]{2,1,0:T(8,128)(2,1)S(1)} collective-permute-done((bf16[5,128,128]{2,1,0:T(8,128)(2,1)S(1)}, bf16[5,128,128]{2,1,0:T(8,128)(2,1)S(1)}, u32[]{:S(2)}, u32[]{:S(2)}) %collective-permute-start.7) | collective-permute-done | bytes 163872 | tf_op jit(solution)/shard_map/ppermute | solution.py:292
  34.3 1.1 %collective-permute-start.11 = (bf16[5,128,128]{2,1,0:T(8,128)(2,1)S(1)}, bf16[5,128,128]{2,1,0:T(8,128)(2,1)S(1)}, u32[]{:S(2)}, u32[]{:S(2)}) collective-permute-start(bf16[5,128,128]{2,1,0:T(8,128)(2,1)S(1)} %get-tuple-element.22), channel_id=1, source_target_pairs={{0,1},{1,0},{2,3},{3,2},{4,5},{5,4},{6,7},{7,6},{8,9},{9,8},{10,11... | collective-permute-start | bytes 491528 | tf_op jit(solution)/shard_map/ppermute | solution.py:295
  35.3 0.0 collective-permute-start.10
  35.3 1.6 %collective-permute-start.9 = (bf16[5,128,128]{2,1,0:T(8,128)(2,1)S(1)}, bf16[5,128,128]{2,1,0:T(8,128)(2,1)S(1)}, u32[]{:S(2)}, u32[]{:S(2)}) collective-permute-start(bf16[5,128,128]{2,1,0:T(8,128)(2,1)S(1)} %get-tuple-element.21.refs_0_), channel_id=1, source_target_pairs={{0,8},{2,10},{4,12},{6,14},{8,0},{10,2},{12,4},{14,6},{16,24},{18,... | collective-permute-start | bytes 491528 | tf_op jit(solution)/shard_map/ppermute | solution.py:292
  36.9 1.9 %collective-permute-start.8 = (bf16[5,128,128]{2,1,0:T(8,128)(2,1)S(1)}, bf16[5,128,128]{2,1,0:T(8,128)(2,1)S(1)}, u32[]{:S(2)}, u32[]{:S(2)}) collective-permute-start(bf16[5,128,128]{2,1,0:T(8,128)(2,1)S(1)} %get-tuple-element.21.refs_0_), channel_id=1, source_target_pairs={{0,4},{2,6},{4,0},{6,2},{8,12},{10,14},{12,8},{14,10},{16,20},{18,... | collective-permute-start | bytes 491528 | tf_op jit(solution)/shard_map/ppermute | solution.py:292
  38.8 1.5 %collective-permute-done.11.refs_0_ = bf16[5,128,128]{2,1,0:T(8,128)(2,1)S(1)} collective-permute-done((bf16[5,128,128]{2,1,0:T(8,128)(2,1)S(1)}, bf16[5,128,128]{2,1,0:T(8,128)(2,1)S(1)}, u32[]{:S(2)}, u32[]{:S(2)}) %collective-permute-start.11) | collective-permute-done | bytes 163872 | tf_op jit(solution)/shard_map/ppermute | solution.py:295
  40.3 0.0 collective-permute-start.14
  40.3 0.4 collective-permute-start.13
  40.7 2.6 %collective-permute-done.10.refs_3_ = bf16[5,128,128]{2,1,0:T(8,128)(2,1)S(1)} collective-permute-done((bf16[5,128,128]{2,1,0:T(8,128)(2,1)S(1)}, bf16[5,128,128]{2,1,0:T(8,128)(2,1)S(1)}, u32[]{:S(2)}, u32[]{:S(2)}) %collective-permute-start.10) | collective-permute-done | bytes 163872 | tf_op jit(solution)/shard_map/ppermute | solution.py:292
  43.3 0.5 collective-permute-start.12
  43.8 1.4 %collective-permute-done.9.refs_2_ = bf16[5,128,128]{2,1,0:T(8,128)(2,1)S(1)} collective-permute-done((bf16[5,128,128]{2,1,0:T(8,128)(2,1)S(1)}, bf16[5,128,128]{2,1,0:T(8,128)(2,1)S(1)}, u32[]{:S(2)}, u32[]{:S(2)}) %collective-permute-start.9) | collective-permute-done | bytes 163872 | tf_op jit(solution)/shard_map/ppermute | solution.py:292
  45.2 2.5 %collective-permute-done.8.refs_1_ = bf16[5,128,128]{2,1,0:T(8,128)(2,1)S(1)} collective-permute-done((bf16[5,128,128]{2,1,0:T(8,128)(2,1)S(1)}, bf16[5,128,128]{2,1,0:T(8,128)(2,1)S(1)}, u32[]{:S(2)}, u32[]{:S(2)}) %collective-permute-start.8) | collective-permute-done | bytes 163872 | tf_op jit(solution)/shard_map/ppermute | solution.py:292
  47.8 0.1 collective-permute-start.15
  47.9 2.2 %collective-permute-done.14.refs_3_ = bf16[5,128,128]{2,1,0:T(8,128)(2,1)S(1)} collective-permute-done((bf16[5,128,128]{2,1,0:T(8,128)(2,1)S(1)}, bf16[5,128,128]{2,1,0:T(8,128)(2,1)S(1)}, u32[]{:S(2)}, u32[]{:S(2)}) %collective-permute-start.14) | collective-permute-done | bytes 163872 | tf_op jit(solution)/shard_map/ppermute | solution.py:292
  50.1 0.0 collective-permute-done.13.refs_2_
  50.1 1.7 %collective-permute-done.12.refs_1_ = bf16[5,128,128]{2,1,0:T(8,128)(2,1)S(1)} collective-permute-done((bf16[5,128,128]{2,1,0:T(8,128)(2,1)S(1)}, bf16[5,128,128]{2,1,0:T(8,128)(2,1)S(1)}, u32[]{:S(2)}, u32[]{:S(2)}) %collective-permute-start.12) | collective-permute-done | bytes 163872 | tf_op jit(solution)/shard_map/ppermute | solution.py:292
  51.9 0.1 collective-permute-start.16
  52.0 0.0 collective-permute-done.15.home_core_ref
  52.0 0.1 own_collected.1.rest_0_
  52.1 1.9 %collective-permute-done.16.rest_1_ = bf16[20,128,128]{2,1,0:T(8,128)(2,1)S(1)} collective-permute-done((bf16[20,128,128]{2,1,0:T(8,128)(2,1)S(1)}, bf16[20,128,128]{2,1,0:T(8,128)(2,1)S(1)}, u32[]{:S(2)}, u32[]{:S(2)}) %collective-permute-start.16) | collective-permute-done | bytes 655392 | tf_op jit(solution)/shard_map/ppermute | solution.py:292
  54.1 1.5 %second_layer.2 = (bf16[5,128,128]{2,1,0:T(8,128)(2,1)S(1)}, bf16[80,128,128]{2,1,0:T(8,128)(2,1)S(1)}) custom-call(s32[10,36]{1,0:T(8,128)S(1)} %copy-done.1, s32[10]{0:T(128)S(1)} %bitcast.13, bf16[10,36,128,128]{3,2,1,0:T(8,128)(2,1)S(1)} %get-tuple-element.18.coef_ref, ...), custom_call_target="tpu_custom_call", output_to_operand_aliasing={{1}: (4, {})} | custom-call | flops 754974720 | bytes 5898240 | tf_op jit(solution)/shard_map/second_layer/pallas_call | solution.py:347
  55.5 1.7 %collective-permute-start.18 = (bf16[5,128,128]{2,1,0:T(8,128)(2,1)S(1)}, bf16[5,128,128]{2,1,0:T(8,128)(2,1)S(1)}, u32[]{:S(2)}, u32[]{:S(2)}) collective-permute-start(bf16[5,128,128]{2,1,0:T(8,128)(2,1)S(1)} %get-tuple-element.24.mine_ref), channel_id=1, source_target_pairs={{0,1},{1,0},{2,3},{3,2},{4,5},{5,4},{6,7},{7,6},{8,9},{9,8},{10,11... | collective-permute-start | bytes 491528 | tf_op jit(solution)/shard_map/ppermute | solution.py:295
  57.3 1.8 %second_layer.3.mine_ref = bf16[5,128,128]{2,1,0:T(8,128)(2,1)S(1)} custom-call(s32[10,36]{1,0:T(8,128)S(1)} %copy-done.1, s32[10]{0:T(128)S(1)} %bitcast.14, bf16[10,36,128,128]{3,2,1,0:T(8,128)(2,1)S(1)} %get-tuple-element.18.coef_ref, bf16[5,128,128]{2,1,0:T(8,128)(2,1)S(1)} %add_convert_fusion.own_ref, bf16[80,128,128]{2,1,0:T(8,128)(2,1)S(1)} %get-tuple-element.23.rest_0_), custom_call_target="tpu_custom_call" | custom-call | flops 754974720 | bytes 5898240 | tf_op jit(solution)/shard_map/second_layer/pallas_call | solution.py:347
  59.1 0.4 collective-permute-start.17
  59.5 2.5 %collective-permute-done.18.other_ref = bf16[5,128,128]{2,1,0:T(8,128)(2,1)S(1)} collective-permute-done((bf16[5,128,128]{2,1,0:T(8,128)(2,1)S(1)}, bf16[5,128,128]{2,1,0:T(8,128)(2,1)S(1)}, u32[]{:S(2)}, u32[]{:S(2)}) %collective-permute-start.18) | collective-permute-done | bytes 163872 | tf_op jit(solution)/shard_map/ppermute | solution.py:295
  62.0 0.7 %result.2.rest_0_ = bf16[10,128,128]{2,1,0:T(8,128)(2,1)} custom-call(bf16[5,128,128]{2,1,0:T(8,128)(2,1)S(1)} %get-tuple-element.24.mine_ref, bf16[5,128,128]{2,1,0:T(8,128)(2,1)S(1)} %collective-permute-done.18.other_ref), custom_call_target="tpu_custom_call" | custom-call | tf_op jit(solution)/shard_map/result/pallas_call | solution.py:425
  62.8 2.6 %collective-permute-done.17.other_ref = bf16[5,128,128]{2,1,0:T(8,128)(2,1)S(1)} collective-permute-done((bf16[5,128,128]{2,1,0:T(8,128)(2,1)S(1)}, bf16[5,128,128]{2,1,0:T(8,128)(2,1)S(1)}, u32[]{:S(2)}, u32[]{:S(2)}) %collective-permute-start.17) | collective-permute-done | bytes 163872 | tf_op jit(solution)/shard_map/ppermute | solution.py:295
  65.4 0.7 %result.3 = bf16[10,128,128]{2,1,0:T(8,128)(2,1)} custom-call(bf16[5,128,128]{2,1,0:T(8,128)(2,1)S(1)} %second_layer.3.mine_ref, bf16[5,128,128]{2,1,0:T(8,128)(2,1)S(1)} %collective-permute-done.17.other_ref, bf16[10,128,128]{2,1,0:T(8,128)(2,1)} %result.2.rest_0_), custom_call_target="tpu_custom_call", output_to_operand_aliasing={{}: (2, {})} | custom-call | tf_op jit(solution)/shard_map/result/pallas_call | solution.py:425
  (7 shorter events, 0.2 us)
Async XLA Ops:
  0.0 18.3 %copy-start.1 = (s32[10,36]{1,0:T(8,128)S(1)}, s32[10,36]{1,0:T(8,128)}, u32[]{:S(2)}) copy-start(s32[10,36]{1,0:T(8,128)} %cols_ref.9) | copy-start | bytes 4324
  0.0 18.3 %copy-start.2 = (s32[10,1]{0,1:T(1,128)S(1)}, s32[10,1]{0,1:T(1,128)}, u32[]{:S(2)}) copy-start(s32[10,1]{0,1:T(1,128)} %param.7) | copy-start | bytes 124
  0.0 18.4 %copy-start = (f32[10240]{0:T(1024)S(1)}, f32[10240]{0:T(1024)}, u32[]{:S(2)}) copy-start(f32[10240]{0:T(1024)} %param.9) | copy-start | bytes 122884
  3.0 4.5 %collective-permute-start.1 = (bf16[80,128]{1,0:T(8,128)(2,1)S(1)}, bf16[80,128]{1,0:T(8,128)(2,1)S(1)}, u32[]{:S(2)}, u32[]{:S(2)}) collective-permute-start(bf16[80,128]{1,0:T(8,128)(2,1)S(1)} %convert_element_type.36), channel_id=1, source_target_pairs={{0,4},{2,6},{4,0},{6,2},{8,12},{10,14},{12,8},{14,10},{16,20},{18,... | collective-permute-start | bytes 61448 | tf_op jit(solution)/shard_map/ppermute | solution.py:292
  5.7 1.8 %collective-permute-start = (bf16[80,128]{1,0:T(8,128)(2,1)S(1)}, bf16[80,128]{1,0:T(8,128)(2,1)S(1)}, u32[]{:S(2)}, u32[]{:S(2)}) collective-permute-start(bf16[80,128]{1,0:T(8,128)(2,1)S(1)} %convert_element_type.36), channel_id=1, source_target_pairs={{0,2},{2,0},{4,6},{6,4},{8,10},{10,8},{12,14},{14,12},{16,18},{18,... | collective-permute-start | bytes 61448 | tf_op jit(solution)/shard_map/ppermute | solution.py:292
  5.9 3.2 %collective-permute-start.2 = (bf16[80,128]{1,0:T(8,128)(2,1)S(1)}, bf16[80,128]{1,0:T(8,128)(2,1)S(1)}, u32[]{:S(2)}, u32[]{:S(2)}) collective-permute-start(bf16[80,128]{1,0:T(8,128)(2,1)S(1)} %convert_element_type.36), channel_id=1, source_target_pairs={{0,6},{2,4},{4,2},{6,0},{8,14},{10,12},{12,10},{14,8},{16,22},{18,... | collective-permute-start | bytes 61448 | tf_op jit(solution)/shard_map/ppermute | solution.py:292
  9.1 6.9 %collective-permute-start.5 = (bf16[80,128]{1,0:T(8,128)(2,1)S(1)}, bf16[80,128]{1,0:T(8,128)(2,1)S(1)}, u32[]{:S(2)}, u32[]{:S(2)}) collective-permute-start(bf16[80,128]{1,0:T(8,128)(2,1)S(1)} %add_convert_fusion.1._), channel_id=1, source_target_pairs={{0,24},{2,26},{4,28},{6,30},{8,16},{10,18},{12,20},{14,22},{16,8},... | collective-permute-start | bytes 61448 | tf_op jit(solution)/shard_map/ppermute | solution.py:292
  13.6 4.7 %collective-permute-start.4 = (bf16[80,128]{1,0:T(8,128)(2,1)S(1)}, bf16[80,128]{1,0:T(8,128)(2,1)S(1)}, u32[]{:S(2)}, u32[]{:S(2)}) collective-permute-start(bf16[80,128]{1,0:T(8,128)(2,1)S(1)} %add_convert_fusion.1._), channel_id=1, source_target_pairs={{0,16},{2,18},{4,20},{6,22},{8,24},{10,26},{12,28},{14,30},{16,0},... | collective-permute-start | bytes 61448 | tf_op jit(solution)/shard_map/ppermute | solution.py:292
  13.6 4.7 %collective-permute-start.3 = (bf16[80,128]{1,0:T(8,128)(2,1)S(1)}, bf16[80,128]{1,0:T(8,128)(2,1)S(1)}, u32[]{:S(2)}, u32[]{:S(2)}) collective-permute-start(bf16[80,128]{1,0:T(8,128)(2,1)S(1)} %add_convert_fusion.1._), channel_id=1, source_target_pairs={{0,8},{2,10},{4,12},{6,14},{8,0},{10,2},{12,4},{14,6},{16,24},{18,... | collective-permute-start | bytes 61448 | tf_op jit(solution)/shard_map/ppermute | solution.py:292
  20.2 5.4 %collective-permute-start.6 = (bf16[5,128,128]{2,1,0:T(8,128)(2,1)S(1)}, bf16[5,128,128]{2,1,0:T(8,128)(2,1)S(1)}, u32[]{:S(2)}, u32[]{:S(2)}) collective-permute-start(bf16[5,128,128]{2,1,0:T(8,128)(2,1)S(1)} %first_layer.2.rest_0_), channel_id=1, source_target_pairs={{0,1},{1,0},{2,3},{3,2},{4,5},{5,4},{6,7},{7,6},{8,9},{9,8},{10,11... | collective-permute-start | bytes 491528 | tf_op jit(solution)/shard_map/ppermute | solution.py:295
  25.7 8.6 %collective-permute-start.7 = (bf16[5,128,128]{2,1,0:T(8,128)(2,1)S(1)}, bf16[5,128,128]{2,1,0:T(8,128)(2,1)S(1)}, u32[]{:S(2)}, u32[]{:S(2)}) collective-permute-start(bf16[5,128,128]{2,1,0:T(8,128)(2,1)S(1)} %add_convert_fusion.own_ref), channel_id=1, source_target_pairs={{0,16},{2,18},{4,20},{6,22},{8,24},{10,26},{12,28},{14,30},{16,0},... | collective-permute-start | bytes 491528 | tf_op jit(solution)/shard_map/ppermute | solution.py:292
  34.3 6.0 %collective-permute-start.11 = (bf16[5,128,128]{2,1,0:T(8,128)(2,1)S(1)}, bf16[5,128,128]{2,1,0:T(8,128)(2,1)S(1)}, u32[]{:S(2)}, u32[]{:S(2)}) collective-permute-start(bf16[5,128,128]{2,1,0:T(8,128)(2,1)S(1)} %get-tuple-element.22), channel_id=1, source_target_pairs={{0,1},{1,0},{2,3},{3,2},{4,5},{5,4},{6,7},{7,6},{8,9},{9,8},{10,11... | collective-permute-start | bytes 491528 | tf_op jit(solution)/shard_map/ppermute | solution.py:295
  35.3 8.0 %collective-permute-start.10 = (bf16[5,128,128]{2,1,0:T(8,128)(2,1)S(1)}, bf16[5,128,128]{2,1,0:T(8,128)(2,1)S(1)}, u32[]{:S(2)}, u32[]{:S(2)}) collective-permute-start(bf16[5,128,128]{2,1,0:T(8,128)(2,1)S(1)} %get-tuple-element.21.refs_0_), channel_id=1, source_target_pairs={{0,12},{2,14},{4,8},{6,10},{8,4},{10,6},{12,0},{14,2},{16,28},{18,... | collective-permute-start | bytes 491528 | tf_op jit(solution)/shard_map/ppermute | solution.py:292
  35.3 9.9 %collective-permute-start.9 = (bf16[5,128,128]{2,1,0:T(8,128)(2,1)S(1)}, bf16[5,128,128]{2,1,0:T(8,128)(2,1)S(1)}, u32[]{:S(2)}, u32[]{:S(2)}) collective-permute-start(bf16[5,128,128]{2,1,0:T(8,128)(2,1)S(1)} %get-tuple-element.21.refs_0_), channel_id=1, source_target_pairs={{0,8},{2,10},{4,12},{6,14},{8,0},{10,2},{12,4},{14,6},{16,24},{18,... | collective-permute-start | bytes 491528 | tf_op jit(solution)/shard_map/ppermute | solution.py:292
  36.9 10.8 %collective-permute-start.8 = (bf16[5,128,128]{2,1,0:T(8,128)(2,1)S(1)}, bf16[5,128,128]{2,1,0:T(8,128)(2,1)S(1)}, u32[]{:S(2)}, u32[]{:S(2)}) collective-permute-start(bf16[5,128,128]{2,1,0:T(8,128)(2,1)S(1)} %get-tuple-element.21.refs_0_), channel_id=1, source_target_pairs={{0,4},{2,6},{4,0},{6,2},{8,12},{10,14},{12,8},{14,10},{16,20},{18,... | collective-permute-start | bytes 491528 | tf_op jit(solution)/shard_map/ppermute | solution.py:292
  40.3 9.8 %collective-permute-start.14 = (bf16[5,128,128]{2,1,0:T(8,128)(2,1)S(1)}, bf16[5,128,128]{2,1,0:T(8,128)(2,1)S(1)}, u32[]{:S(2)}, u32[]{:S(2)}) collective-permute-start(bf16[5,128,128]{2,1,0:T(8,128)(2,1)S(1)} %collective-permute-done.11.refs_0_), channel_id=1, source_target_pairs={{0,12},{2,14},{4,8},{6,10},{8,4},{10,6},{12,0},{14,2},{16,28},{18,... | collective-permute-start | bytes 491528 | tf_op jit(solution)/shard_map/ppermute | solution.py:292
  40.3 9.8 %collective-permute-start.13 = (bf16[5,128,128]{2,1,0:T(8,128)(2,1)S(1)}, bf16[5,128,128]{2,1,0:T(8,128)(2,1)S(1)}, u32[]{:S(2)}, u32[]{:S(2)}) collective-permute-start(bf16[5,128,128]{2,1,0:T(8,128)(2,1)S(1)} %collective-permute-done.11.refs_0_), channel_id=1, source_target_pairs={{0,8},{2,10},{4,12},{6,14},{8,0},{10,2},{12,4},{14,6},{16,24},{18,... | collective-permute-start | bytes 491528 | tf_op jit(solution)/shard_map/ppermute | solution.py:292
  43.3 8.5 %collective-permute-start.12 = (bf16[5,128,128]{2,1,0:T(8,128)(2,1)S(1)}, bf16[5,128,128]{2,1,0:T(8,128)(2,1)S(1)}, u32[]{:S(2)}, u32[]{:S(2)}) collective-permute-start(bf16[5,128,128]{2,1,0:T(8,128)(2,1)S(1)} %collective-permute-done.11.refs_0_), channel_id=1, source_target_pairs={{0,4},{2,6},{4,0},{6,2},{8,12},{10,14},{12,8},{14,10},{16,20},{18,... | collective-permute-start | bytes 491528 | tf_op jit(solution)/shard_map/ppermute | solution.py:292
  47.8 4.2 %collective-permute-start.15 = (bf16[20,128,128]{2,1,0:T(8,128)(2,1)S(1)}, bf16[20,128,128]{2,1,0:T(8,128)(2,1)S(1)}, u32[]{:S(2)}, u32[]{:S(2)}) collective-permute-start(bf16[20,128,128]{2,1,0:T(8,128)(2,1)S(1)} %own_joined.2.home_ref), channel_id=1, source_target_pairs={{0,2},{2,0},{4,6},{6,4},{8,10},{10,8},{12,14},{14,12},{16,18},{18,... | collective-permute-start | bytes 1966088 | tf_op jit(solution)/shard_map/ppermute | solution.py:292
  51.9 2.2 %collective-permute-start.16 = (bf16[20,128,128]{2,1,0:T(8,128)(2,1)S(1)}, bf16[20,128,128]{2,1,0:T(8,128)(2,1)S(1)}, u32[]{:S(2)}, u32[]{:S(2)}) collective-permute-start(bf16[20,128,128]{2,1,0:T(8,128)(2,1)S(1)} %own_joined.3.away_ref), channel_id=1, source_target_pairs={{0,2},{2,0},{4,6},{6,4},{8,10},{10,8},{12,14},{14,12},{16,18},{18,... | collective-permute-start | bytes 1966088 | tf_op jit(solution)/shard_map/ppermute | solution.py:292
  55.5 6.5 %collective-permute-start.18 = (bf16[5,128,128]{2,1,0:T(8,128)(2,1)S(1)}, bf16[5,128,128]{2,1,0:T(8,128)(2,1)S(1)}, u32[]{:S(2)}, u32[]{:S(2)}) collective-permute-start(bf16[5,128,128]{2,1,0:T(8,128)(2,1)S(1)} %get-tuple-element.24.mine_ref), channel_id=1, source_target_pairs={{0,1},{1,0},{2,3},{3,2},{4,5},{5,4},{6,7},{7,6},{8,9},{9,8},{10,11... | collective-permute-start | bytes 491528 | tf_op jit(solution)/shard_map/ppermute | solution.py:295
  59.1 6.3 %collective-permute-start.17 = (bf16[5,128,128]{2,1,0:T(8,128)(2,1)S(1)}, bf16[5,128,128]{2,1,0:T(8,128)(2,1)S(1)}, u32[]{:S(2)}, u32[]{:S(2)}) collective-permute-start(bf16[5,128,128]{2,1,0:T(8,128)(2,1)S(1)} %second_layer.3.mine_ref), channel_id=1, source_target_pairs={{0,1},{1,0},{2,3},{3,2},{4,5},{5,4},{6,7},{7,6},{8,9},{9,8},{10,11... | collective-permute-start | bytes 491528 | tf_op jit(solution)/shard_map/ppermute | solution.py:295
where the time goes:
time: 66.1 us
  waiting for transfers between devices  31 us (47%)
  starting transfers between devices  19.8 us (30%)
  Pallas kernels  15 us (23%)
    ppermute x15, waiting for transfers between devices, flip(): return lax.ppermute(array, 'row', [(i, i ^ mask) for i in range(n_row)])  22.2 us
    ppermute x15, starting transfers between devices, flip(): return lax.ppermute(array, 'row', [(i, i ^ mask) for i in range(n_row)])  15.4 us
    ppermute x4, waiting for transfers between devices, swap(): return lax.ppermute(array, 'col', [(0, 1), (1, 0)])  8.8 us
    ppermute x4, starting transfers between devices, swap(): return lax.ppermute(array, 'col', [(0, 1), (1, 0)])  4.41 us
    pallas_call x2, Pallas kernels, first_layer(): pl.pallas_call(functools.partial(first_kernel, sending), name='first_laye...  3.84 us
    pallas_call x2, Pallas kernels, second_call(): pl.pallas_call(kernel, name='second_layer', out_shape=(out, pltpu.VMEM((g...  3.31 us
    pallas_call x1, Pallas kernels, body(): pl.pallas_call(sums_kernel, name='column_sums', out_shape=(jax.ShapeDtype...  2.99 us
    pallas_call x1, Pallas kernels, body(): pl.pallas_call(fetch_kernel, name='own_demand', out_shape=pltpu.VMEM(dema...  1.75 us
  transfers between devices with their start and end apart: 19, of which 14 were waited for; matrix products, arithmetic and copies ran while one was open for 0% of the time, Pallas kernels for 12%

commit v1 on v0

--- a/solution.py
+++ b/solution.py
@@ -295,7 +295,7 @@
         return lax.ppermute(array, "col", [(0, 1), (1, 0)])
 
     if paired:
-        for masks in ((1, 2, 3), (4, 8, 12)):
+        for masks in ((1, 2, 3), (4, 12, 8)):
             sums = sums.astype(jnp.bfloat16)
             parts = [sums] + [flip(sums, m) for m in masks]
             if masks[0] == 4:

time: 66.1 us -> 65.2 us (0.986)
  waiting for transfers between devices: 31 us -> 26.4 us
  Pallas kernels: 15 us -> 16.9 us
  starting transfers between devices: 19.8 us -> 21.6 us
    ppermute x4, waiting for transfers between devices: 8.8 us -> 5.44 us  [swap(): return lax.ppermute(array, 'col', [(0, 1), (1, 0)])]
    ppermute x15, waiting for transfers between devices: 22.2 us -> 20.9 us  [flip(): return lax.ppermute(array, 'row', [(i, i ^ mask) for i in range(n_row)])]
    ppermute x4, starting transfers between devices: 4.41 us -> 5.63 us  [swap(): return lax.ppermute(array, 'col', [(0, 1), (1, 0)])]
    pallas_call x2, Pallas kernels: 3.84 us -> 4.58 us  [first_layer(): pl.pallas_call(functools.partial(first_kernel, sending), name='first_laye...]
    pallas_call x2, Pallas kernels: 3.31 us -> 4.05 us  [second_call(): pl.pallas_call(kernel, name='second_layer', out_shape=(out, pltpu.VMEM((g...]
  transfers between devices with their start and end apart: 19 -> 19, of which waited for: 14 -> 15; matrix products, arithmetic and copies ran while one was open for 0% -> 0% of each run, Pallas kernels for 12% -> 13%
where the time goes in v1:
time: 65.2 us; the launch traced here: 65.1 us
  waiting for transfers between devices  26.4 us (40%)
  starting transfers between devices  21.6 us (33%)
  Pallas kernels  16.9 us (26%)
    ppermute x15, waiting for transfers between devices, flip(): return lax.ppermute(array, 'row', [(i, i ^ mask) for i in range(n_row)])  20.9 us
    ppermute x15, starting transfers between devices, flip(): return lax.ppermute(array, 'row', [(i, i ^ mask) for i in range(n_row)])  15.9 us
    ppermute x4, starting transfers between devices, swap(): return lax.ppermute(array, 'col', [(0, 1), (1, 0)])  5.63 us
    ppermute x4, waiting for transfers between devices, swap(): return lax.ppermute(array, 'col', [(0, 1), (1, 0)])  5.44 us
    pallas_call x2, Pallas kernels, first_layer(): pl.pallas_call(functools.partial(first_kernel, sending), name='first_laye...  4.58 us
    pallas_call x2, Pallas kernels, second_call(): pl.pallas_call(kernel, name='second_layer', out_shape=(out, pltpu.VMEM((g...  4.05 us
    pallas_call x1, Pallas kernels, body(): pl.pallas_call(sums_kernel, name='column_sums', out_shape=(jax.ShapeDtype...  3.45 us
    pallas_call x1, Pallas kernels, body(): pl.pallas_call(fetch_kernel, name='own_demand', out_shape=pltpu.VMEM(dema...  1.75 us
  transfers between devices with their start and end apart: 19, of which 15 were waited for; matrix products, arithmetic and copies ran while one was open for 0% of the time, Pallas kernels for 13%

profile of v1, /device:TPU:0, one launch (start us, length us, event | category | flops | bytes accessed | tf_op | source)
XLA Modules:
  0.0 65.1 jit_solution(18261725008623569694)
XLA Ops:
  0.0 0.0 copy-start.1
  0.0 0.0 copy-start.2
  0.0 0.0 copy-start
  0.0 3.5 %column_sums.1 = (f32[80,128]{1,0:T(8,128)S(1)}, bf16[10,36,128,128]{3,2,1,0:T(8,128)(2,1)S(1)}) custom-call(s32[10,36]{1,0:T(8,128)} %cols_ref.9, s32[10]{0:T(128)} %bitcast.9, bf16[10,36,128,128]{3,2,1,0:T(8,128)(2,1)} %blocks_ref.1), custom_call_target="tpu_custom_call" | custom-call | bytes 23592960 | tf_op jit(solution)/shard_map/column_sums/pallas_call | solution.py:271
  3.5 2.6 %collective-permute-start.1 = (bf16[80,128]{1,0:T(8,128)(2,1)S(1)}, bf16[80,128]{1,0:T(8,128)(2,1)S(1)}, u32[]{:S(2)}, u32[]{:S(2)}) collective-permute-start(bf16[80,128]{1,0:T(8,128)(2,1)S(1)} %convert_element_type.36), channel_id=1, source_target_pairs={{0,4},{2,6},{4,0},{6,2},{8,12},{10,14},{12,8},{14,10},{16,20},{18,... | collective-permute-start | bytes 61448 | tf_op jit(solution)/shard_map/ppermute | solution.py:292
  6.1 0.0 collective-permute-start
  6.1 0.2 collective-permute-start.2
  6.3 1.6 %collective-permute-done.1 = bf16[80,128]{1,0:T(8,128)(2,1)S(1)} collective-permute-done((bf16[80,128]{1,0:T(8,128)(2,1)S(1)}, bf16[80,128]{1,0:T(8,128)(2,1)S(1)}, u32[]{:S(2)}, u32[]{:S(2)}) %collective-permute-start.1) | collective-permute-done | bytes 20512 | tf_op jit(solution)/shard_map/ppermute | solution.py:292
  7.8 0.0 collective-permute-done
  7.8 1.4 %collective-permute-done.2 = bf16[80,128]{1,0:T(8,128)(2,1)S(1)} collective-permute-done((bf16[80,128]{1,0:T(8,128)(2,1)S(1)}, bf16[80,128]{1,0:T(8,128)(2,1)S(1)}, u32[]{:S(2)}, u32[]{:S(2)}) %collective-permute-start.2) | collective-permute-done | bytes 20512 | tf_op jit(solution)/shard_map/ppermute | solution.py:292
  9.3 3.1 %collective-permute-start.5 = (bf16[80,128]{1,0:T(8,128)(2,1)S(1)}, bf16[80,128]{1,0:T(8,128)(2,1)S(1)}, u32[]{:S(2)}, u32[]{:S(2)}) collective-permute-start(bf16[80,128]{1,0:T(8,128)(2,1)S(1)} %add_convert_fusion.1._), channel_id=1, source_target_pairs={{0,16},{2,18},{4,20},{6,22},{8,24},{10,26},{12,28},{14,30},{16,0},... | collective-permute-start | bytes 61448 | tf_op jit(solution)/shard_map/ppermute | solution.py:292
  12.4 1.1 %collective-permute-start.4 = (bf16[80,128]{1,0:T(8,128)(2,1)S(1)}, bf16[80,128]{1,0:T(8,128)(2,1)S(1)}, u32[]{:S(2)}, u32[]{:S(2)}) collective-permute-start(bf16[80,128]{1,0:T(8,128)(2,1)S(1)} %add_convert_fusion.1._), channel_id=1, source_target_pairs={{0,24},{2,26},{4,28},{6,30},{8,16},{10,18},{12,20},{14,22},{16,8},... | collective-permute-start | bytes 61448 | tf_op jit(solution)/shard_map/ppermute | solution.py:292
  13.5 0.0 collective-permute-start.3
  13.5 1.7 %own_demand.1 = bf16[10240,128]{1,0:T(8,128)(2,1)S(1)} custom-call(bf16[10240,128]{1,0:T(8,128)(2,1)} %demand_hbm.1, bf16[80,128]{1,0:T(8,128)(2,1)S(1)} %add_convert_fusion.1._), custom_call_target="tpu_custom_call" | custom-call | bytes 7864320 | tf_op jit(solution)/shard_map/own_demand/pallas_call | solution.py:302
  15.3 0.0 collective-permute-done.5
  15.3 2.7 %collective-permute-done.4 = bf16[80,128]{1,0:T(8,128)(2,1)S(1)} collective-permute-done((bf16[80,128]{1,0:T(8,128)(2,1)S(1)}, bf16[80,128]{1,0:T(8,128)(2,1)S(1)}, u32[]{:S(2)}, u32[]{:S(2)}) %collective-permute-start.4) | collective-permute-done | bytes 20512 | tf_op jit(solution)/shard_map/ppermute | solution.py:292
  18.0 0.0 collective-permute-done.3
  18.0 0.0 copy-done.1
  18.0 0.0 copy-done.2
  18.1 0.0 copy-done
  18.1 1.9 %first_layer.2.rest_0_ = bf16[5,128,128]{2,1,0:T(8,128)(2,1)S(1)} custom-call(s32[10,36]{1,0:T(8,128)S(1)} %copy-done.1, s32[10]{0:T(128)S(1)} %bitcast.10, f32[80,128]{1,0:T(8,128)S(1)} %convert_add_fusion.sums_ref, f32[80,128]{1,0:T(8,128)S(1)} %bitcast.6, bf16[80,128,128]{2,1,0:T(8,128)(2,1)S(1)} %bitcast.4, ...), custom_call_target="tpu_custom_call" | custom-call | flops 754974720 | bytes 5898240 | tf_op jit(solution)/shard_map/first_layer/pallas_call | solution.py:321
  19.9 1.9 %collective-permute-start.6 = (bf16[5,128,128]{2,1,0:T(8,128)(2,1)S(1)}, bf16[5,128,128]{2,1,0:T(8,128)(2,1)S(1)}, u32[]{:S(2)}, u32[]{:S(2)}) collective-permute-start(bf16[5,128,128]{2,1,0:T(8,128)(2,1)S(1)} %first_layer.2.rest_0_), channel_id=1, source_target_pairs={{0,1},{1,0},{2,3},{3,2},{4,5},{5,4},{6,7},{7,6},{8,9},{9,8},{10,11... | collective-permute-start | bytes 491528 | tf_op jit(solution)/shard_map/ppermute | solution.py:295
  21.9 2.7 %first_layer.3 = (f32[5,128,128]{2,1,0:T(8,128)S(1)}, bf16[10,36,128,128]{3,2,1,0:T(8,128)(2,1)S(1)}) custom-call(s32[10,36]{1,0:T(8,128)S(1)} %copy-done.1, s32[10]{0:T(128)S(1)} %bitcast.11, f32[80,128]{1,0:T(8,128)S(1)} %convert_add_fusion.sums_ref, f32[80,128]{1,0:T(8,128)S(1)} %bitcast.7, ...), custom_call_target="tpu_custom_call", output_to_operand_aliasing={{1}: (5, {})} | custom-call | flops 754974720 | bytes 5898240 | tf_op jit(solution)/shard_map/first_layer/pallas_call | solution.py:321
  24.6 0.7 %collective-permute-done.6 = bf16[5,128,128]{2,1,0:T(8,128)(2,1)S(1)} collective-permute-done((bf16[5,128,128]{2,1,0:T(8,128)(2,1)S(1)}, bf16[5,128,128]{2,1,0:T(8,128)(2,1)S(1)}, u32[]{:S(2)}, u32[]{:S(2)}) %collective-permute-start.6) | collective-permute-done | bytes 163872 | tf_op jit(solution)/shard_map/ppermute | solution.py:295
  25.4 1.1 %collective-permute-start.7 = (bf16[5,128,128]{2,1,0:T(8,128)(2,1)S(1)}, bf16[5,128,128]{2,1,0:T(8,128)(2,1)S(1)}, u32[]{:S(2)}, u32[]{:S(2)}) collective-permute-start(bf16[5,128,128]{2,1,0:T(8,128)(2,1)S(1)} %add_convert_fusion.own_ref), channel_id=1, source_target_pairs={{0,16},{2,18},{4,20},{6,22},{8,24},{10,26},{12,28},{14,30},{16,0},... | collective-permute-start | bytes 491528 | tf_op jit(solution)/shard_map/ppermute | solution.py:292
  26.5 1.4 %own_coefficients.1 = (bf16[10,36,128,128]{3,2,1,0:T(8,128)(2,1)S(1)}, f32[8,128]{1,0:T(8,128)S(1)}) custom-call(s32[10,36]{1,0:T(8,128)S(1)} %copy-done.1, s32[10]{0:T(128)S(1)} %bitcast.12, f32[80,128]{1,0:T(8,128)S(1)} %convert_add_fusion.sums_ref, f32[80,128]{1,0:T(8,128)S(1)} %bitcast.8, ...), custom_call_target="tpu_custom_call", output_to_operand_aliasing={{0}: (4, {})} | custom-call | flops 754974720 | bytes 5898240 | tf_op jit(solution)/shard_map/own_coefficients/pallas_call | solution.py:371
  27.9 5.5 %collective-permute-done.7.crossed_ref = bf16[5,128,128]{2,1,0:T(8,128)(2,1)S(1)} collective-permute-done((bf16[5,128,128]{2,1,0:T(8,128)(2,1)S(1)}, bf16[5,128,128]{2,1,0:T(8,128)(2,1)S(1)}, u32[]{:S(2)}, u32[]{:S(2)}) %collective-permute-start.7) | collective-permute-done | bytes 163872 | tf_op jit(solution)/shard_map/ppermute | solution.py:292
  33.4 1.5 %collective-permute-start.11 = (bf16[5,128,128]{2,1,0:T(8,128)(2,1)S(1)}, bf16[5,128,128]{2,1,0:T(8,128)(2,1)S(1)}, u32[]{:S(2)}, u32[]{:S(2)}) collective-permute-start(bf16[5,128,128]{2,1,0:T(8,128)(2,1)S(1)} %get-tuple-element.22), channel_id=1, source_target_pairs={{0,1},{1,0},{2,3},{3,2},{4,5},{5,4},{6,7},{7,6},{8,9},{9,8},{10,11... | collective-permute-start | bytes 491528 | tf_op jit(solution)/shard_map/ppermute | solution.py:295
  35.0 0.0 collective-permute-start.10
  35.0 2.2 %collective-permute-start.9 = (bf16[5,128,128]{2,1,0:T(8,128)(2,1)S(1)}, bf16[5,128,128]{2,1,0:T(8,128)(2,1)S(1)}, u32[]{:S(2)}, u32[]{:S(2)}) collective-permute-start(bf16[5,128,128]{2,1,0:T(8,128)(2,1)S(1)} %get-tuple-element.21.refs_0_), channel_id=1, source_target_pairs={{0,8},{2,10},{4,12},{6,14},{8,0},{10,2},{12,4},{14,6},{16,24},{18,... | collective-permute-start | bytes 491528 | tf_op jit(solution)/shard_map/ppermute | solution.py:292
  37.1 1.3 %collective-permute-start.8 = (bf16[5,128,128]{2,1,0:T(8,128)(2,1)S(1)}, bf16[5,128,128]{2,1,0:T(8,128)(2,1)S(1)}, u32[]{:S(2)}, u32[]{:S(2)}) collective-permute-start(bf16[5,128,128]{2,1,0:T(8,128)(2,1)S(1)} %get-tuple-element.21.refs_0_), channel_id=1, source_target_pairs={{0,4},{2,6},{4,0},{6,2},{8,12},{10,14},{12,8},{14,10},{16,20},{18,... | collective-permute-start | bytes 491528 | tf_op jit(solution)/shard_map/ppermute | solution.py:292
  38.4 0.3 collective-permute-done.11.refs_0_
  38.8 0.3 collective-permute-start.14
  39.1 3.1 %collective-permute-start.13 = (bf16[5,128,128]{2,1,0:T(8,128)(2,1)S(1)}, bf16[5,128,128]{2,1,0:T(8,128)(2,1)S(1)}, u32[]{:S(2)}, u32[]{:S(2)}) collective-permute-start(bf16[5,128,128]{2,1,0:T(8,128)(2,1)S(1)} %collective-permute-done.11.refs_0_), channel_id=1, source_target_pairs={{0,8},{2,10},{4,12},{6,14},{8,0},{10,2},{12,4},{14,6},{16,24},{18,... | collective-permute-start | bytes 491528 | tf_op jit(solution)/shard_map/ppermute | solution.py:292
  42.3 0.8 %collective-permute-done.10.refs_3_ = bf16[5,128,128]{2,1,0:T(8,128)(2,1)S(1)} collective-permute-done((bf16[5,128,128]{2,1,0:T(8,128)(2,1)S(1)}, bf16[5,128,128]{2,1,0:T(8,128)(2,1)S(1)}, u32[]{:S(2)}, u32[]{:S(2)}) %collective-permute-start.10) | collective-permute-done | bytes 163872 | tf_op jit(solution)/shard_map/ppermute | solution.py:292
  43.1 0.7 %collective-permute-start.12 = (bf16[5,128,128]{2,1,0:T(8,128)(2,1)S(1)}, bf16[5,128,128]{2,1,0:T(8,128)(2,1)S(1)}, u32[]{:S(2)}, u32[]{:S(2)}) collective-permute-start(bf16[5,128,128]{2,1,0:T(8,128)(2,1)S(1)} %collective-permute-done.11.refs_0_), channel_id=1, source_target_pairs={{0,4},{2,6},{4,0},{6,2},{8,12},{10,14},{12,8},{14,10},{16,20},{18,... | collective-permute-start | bytes 491528 | tf_op jit(solution)/shard_map/ppermute | solution.py:292
  43.8 2.0 %collective-permute-done.9.refs_2_ = bf16[5,128,128]{2,1,0:T(8,128)(2,1)S(1)} collective-permute-done((bf16[5,128,128]{2,1,0:T(8,128)(2,1)S(1)}, bf16[5,128,128]{2,1,0:T(8,128)(2,1)S(1)}, u32[]{:S(2)}, u32[]{:S(2)}) %collective-permute-start.9) | collective-permute-done | bytes 163872 | tf_op jit(solution)/shard_map/ppermute | solution.py:292
  45.8 2.0 %collective-permute-done.8.refs_1_ = bf16[5,128,128]{2,1,0:T(8,128)(2,1)S(1)} collective-permute-done((bf16[5,128,128]{2,1,0:T(8,128)(2,1)S(1)}, bf16[5,128,128]{2,1,0:T(8,128)(2,1)S(1)}, u32[]{:S(2)}, u32[]{:S(2)}) %collective-permute-start.8) | collective-permute-done | bytes 163872 | tf_op jit(solution)/shard_map/ppermute | solution.py:292
  47.8 0.1 collective-permute-start.15
  47.9 1.4 %collective-permute-done.14.refs_3_ = bf16[5,128,128]{2,1,0:T(8,128)(2,1)S(1)} collective-permute-done((bf16[5,128,128]{2,1,0:T(8,128)(2,1)S(1)}, bf16[5,128,128]{2,1,0:T(8,128)(2,1)S(1)}, u32[]{:S(2)}, u32[]{:S(2)}) %collective-permute-start.14) | collective-permute-done | bytes 163872 | tf_op jit(solution)/shard_map/ppermute | solution.py:292
  49.3 1.1 %collective-permute-done.13.refs_2_ = bf16[5,128,128]{2,1,0:T(8,128)(2,1)S(1)} collective-permute-done((bf16[5,128,128]{2,1,0:T(8,128)(2,1)S(1)}, bf16[5,128,128]{2,1,0:T(8,128)(2,1)S(1)}, u32[]{:S(2)}, u32[]{:S(2)}) %collective-permute-start.13) | collective-permute-done | bytes 163872 | tf_op jit(solution)/shard_map/ppermute | solution.py:292
  50.4 0.5 collective-permute-done.12.refs_1_
  50.9 0.1 collective-permute-start.16
  51.0 0.0 collective-permute-done.15.home_core_ref
  51.0 0.1 own_collected.1.rest_0_
  51.2 1.9 %collective-permute-done.16.rest_1_ = bf16[20,128,128]{2,1,0:T(8,128)(2,1)S(1)} collective-permute-done((bf16[20,128,128]{2,1,0:T(8,128)(2,1)S(1)}, bf16[20,128,128]{2,1,0:T(8,128)(2,1)S(1)}, u32[]{:S(2)}, u32[]{:S(2)}) %collective-permute-start.16) | collective-permute-done | bytes 655392 | tf_op jit(solution)/shard_map/ppermute | solution.py:292
  53.1 2.2 %second_layer.2 = (bf16[5,128,128]{2,1,0:T(8,128)(2,1)S(1)}, bf16[80,128,128]{2,1,0:T(8,128)(2,1)S(1)}) custom-call(s32[10,36]{1,0:T(8,128)S(1)} %copy-done.1, s32[10]{0:T(128)S(1)} %bitcast.13, bf16[10,36,128,128]{3,2,1,0:T(8,128)(2,1)S(1)} %get-tuple-element.18.coef_ref, ...), custom_call_target="tpu_custom_call", output_to_operand_aliasing={{1}: (4, {})} | custom-call | flops 754974720 | bytes 5898240 | tf_op jit(solution)/shard_map/second_layer/pallas_call | solution.py:347
  55.3 1.0 %collective-permute-start.18 = (bf16[5,128,128]{2,1,0:T(8,128)(2,1)S(1)}, bf16[5,128,128]{2,1,0:T(8,128)(2,1)S(1)}, u32[]{:S(2)}, u32[]{:S(2)}) collective-permute-start(bf16[5,128,128]{2,1,0:T(8,128)(2,1)S(1)} %get-tuple-element.24.mine_ref), channel_id=1, source_target_pairs={{0,1},{1,0},{2,3},{3,2},{4,5},{5,4},{6,7},{7,6},{8,9},{9,8},{10,11... | collective-permute-start | bytes 491528 | tf_op jit(solution)/shard_map/ppermute | solution.py:295
  56.3 1.8 %second_layer.3.mine_ref = bf16[5,128,128]{2,1,0:T(8,128)(2,1)S(1)} custom-call(s32[10,36]{1,0:T(8,128)S(1)} %copy-done.1, s32[10]{0:T(128)S(1)} %bitcast.14, bf16[10,36,128,128]{3,2,1,0:T(8,128)(2,1)S(1)} %get-tuple-element.18.coef_ref, bf16[5,128,128]{2,1,0:T(8,128)(2,1)S(1)} %add_convert_fusion.own_ref, bf16[80,128,128]{2,1,0:T(8,128)(2,1)S(1)} %get-tuple-element.23.rest_0_), custom_call_target="tpu_custom_call" | custom-call | flops 754974720 | bytes 5898240 | tf_op jit(solution)/shard_map/second_layer/pallas_call | solution.py:347
  58.2 1.2 %collective-permute-start.17 = (bf16[5,128,128]{2,1,0:T(8,128)(2,1)S(1)}, bf16[5,128,128]{2,1,0:T(8,128)(2,1)S(1)}, u32[]{:S(2)}, u32[]{:S(2)}) collective-permute-start(bf16[5,128,128]{2,1,0:T(8,128)(2,1)S(1)} %second_layer.3.mine_ref), channel_id=1, source_target_pairs={{0,1},{1,0},{2,3},{3,2},{4,5},{5,4},{6,7},{7,6},{8,9},{9,8},{10,11... | collective-permute-start | bytes 491528 | tf_op jit(solution)/shard_map/ppermute | solution.py:295
  59.3 3.0 %collective-permute-done.18.other_ref = bf16[5,128,128]{2,1,0:T(8,128)(2,1)S(1)} collective-permute-done((bf16[5,128,128]{2,1,0:T(8,128)(2,1)S(1)}, bf16[5,128,128]{2,1,0:T(8,128)(2,1)S(1)}, u32[]{:S(2)}, u32[]{:S(2)}) %collective-permute-start.18) | collective-permute-done | bytes 163872 | tf_op jit(solution)/shard_map/ppermute | solution.py:295
  62.3 0.7 %result.2.rest_0_ = bf16[10,128,128]{2,1,0:T(8,128)(2,1)} custom-call(bf16[5,128,128]{2,1,0:T(8,128)(2,1)S(1)} %get-tuple-element.24.mine_ref, bf16[5,128,128]{2,1,0:T(8,128)(2,1)S(1)} %collective-permute-done.18.other_ref), custom_call_target="tpu_custom_call" | custom-call | tf_op jit(solution)/shard_map/result/pallas_call | solution.py:425
  63.0 1.4 %collective-permute-done.17.other_ref = bf16[5,128,128]{2,1,0:T(8,128)(2,1)S(1)} collective-permute-done((bf16[5,128,128]{2,1,0:T(8,128)(2,1)S(1)}, bf16[5,128,128]{2,1,0:T(8,128)(2,1)S(1)}, u32[]{:S(2)}, u32[]{:S(2)}) %collective-permute-start.17) | collective-permute-done | bytes 163872 | tf_op jit(solution)/shard_map/ppermute | solution.py:295
  64.4 0.7 %result.3 = bf16[10,128,128]{2,1,0:T(8,128)(2,1)} custom-call(bf16[5,128,128]{2,1,0:T(8,128)(2,1)S(1)} %second_layer.3.mine_ref, bf16[5,128,128]{2,1,0:T(8,128)(2,1)S(1)} %collective-permute-done.17.other_ref, bf16[10,128,128]{2,1,0:T(8,128)(2,1)} %result.2.rest_0_), custom_call_target="tpu_custom_call", output_to_operand_aliasing={{}: (2, {})} | custom-call | tf_op jit(solution)/shard_map/result/pallas_call | solution.py:425
  (7 shorter events, 0.2 us)
Async XLA Ops:
  0.0 18.0 %copy-start.1 = (s32[10,36]{1,0:T(8,128)S(1)}, s32[10,36]{1,0:T(8,128)}, u32[]{:S(2)}) copy-start(s32[10,36]{1,0:T(8,128)} %cols_ref.9) | copy-start | bytes 4324
  0.0 18.0 %copy-start.2 = (s32[10,1]{0,1:T(1,128)S(1)}, s32[10,1]{0,1:T(1,128)}, u32[]{:S(2)}) copy-start(s32[10,1]{0,1:T(1,128)} %param.7) | copy-start | bytes 124
  0.0 18.0 %copy-start = (f32[10240]{0:T(1024)S(1)}, f32[10240]{0:T(1024)}, u32[]{:S(2)}) copy-start(f32[10240]{0:T(1024)} %param.9) | copy-start | bytes 122884
  3.5 4.4 %collective-permute-start.1 = (bf16[80,128]{1,0:T(8,128)(2,1)S(1)}, bf16[80,128]{1,0:T(8,128)(2,1)S(1)}, u32[]{:S(2)}, u32[]{:S(2)}) collective-permute-start(bf16[80,128]{1,0:T(8,128)(2,1)S(1)} %convert_element_type.36), channel_id=1, source_target_pairs={{0,4},{2,6},{4,0},{6,2},{8,12},{10,14},{12,8},{14,10},{16,20},{18,... | collective-permute-start | bytes 61448 | tf_op jit(solution)/shard_map/ppermute | solution.py:292
  6.1 1.8 %collective-permute-start = (bf16[80,128]{1,0:T(8,128)(2,1)S(1)}, bf16[80,128]{1,0:T(8,128)(2,1)S(1)}, u32[]{:S(2)}, u32[]{:S(2)}) collective-permute-start(bf16[80,128]{1,0:T(8,128)(2,1)S(1)} %convert_element_type.36), channel_id=1, source_target_pairs={{0,2},{2,0},{4,6},{6,4},{8,10},{10,8},{12,14},{14,12},{16,18},{18,... | collective-permute-start | bytes 61448 | tf_op jit(solution)/shard_map/ppermute | solution.py:292
  6.1 3.2 %collective-permute-start.2 = (bf16[80,128]{1,0:T(8,128)(2,1)S(1)}, bf16[80,128]{1,0:T(8,128)(2,1)S(1)}, u32[]{:S(2)}, u32[]{:S(2)}) collective-permute-start(bf16[80,128]{1,0:T(8,128)(2,1)S(1)} %convert_element_type.36), channel_id=1, source_target_pairs={{0,6},{2,4},{4,2},{6,0},{8,14},{10,12},{12,10},{14,8},{16,22},{18,... | collective-permute-start | bytes 61448 | tf_op jit(solution)/shard_map/ppermute | solution.py:292
  9.3 6.0 %collective-permute-start.5 = (bf16[80,128]{1,0:T(8,128)(2,1)S(1)}, bf16[80,128]{1,0:T(8,128)(2,1)S(1)}, u32[]{:S(2)}, u32[]{:S(2)}) collective-permute-start(bf16[80,128]{1,0:T(8,128)(2,1)S(1)} %add_convert_fusion.1._), channel_id=1, source_target_pairs={{0,16},{2,18},{4,20},{6,22},{8,24},{10,26},{12,28},{14,30},{16,0},... | collective-permute-start | bytes 61448 | tf_op jit(solution)/shard_map/ppermute | solution.py:292
  12.4 5.6 %collective-permute-start.4 = (bf16[80,128]{1,0:T(8,128)(2,1)S(1)}, bf16[80,128]{1,0:T(8,128)(2,1)S(1)}, u32[]{:S(2)}, u32[]{:S(2)}) collective-permute-start(bf16[80,128]{1,0:T(8,128)(2,1)S(1)} %add_convert_fusion.1._), channel_id=1, source_target_pairs={{0,24},{2,26},{4,28},{6,30},{8,16},{10,18},{12,20},{14,22},{16,8},... | collective-permute-start | bytes 61448 | tf_op jit(solution)/shard_map/ppermute | solution.py:292
  13.5 4.5 %collective-permute-start.3 = (bf16[80,128]{1,0:T(8,128)(2,1)S(1)}, bf16[80,128]{1,0:T(8,128)(2,1)S(1)}, u32[]{:S(2)}, u32[]{:S(2)}) collective-permute-start(bf16[80,128]{1,0:T(8,128)(2,1)S(1)} %add_convert_fusion.1._), channel_id=1, source_target_pairs={{0,8},{2,10},{4,12},{6,14},{8,0},{10,2},{12,4},{14,6},{16,24},{18,... | collective-permute-start | bytes 61448 | tf_op jit(solution)/shard_map/ppermute | solution.py:292
  19.9 5.4 %collective-permute-start.6 = (bf16[5,128,128]{2,1,0:T(8,128)(2,1)S(1)}, bf16[5,128,128]{2,1,0:T(8,128)(2,1)S(1)}, u32[]{:S(2)}, u32[]{:S(2)}) collective-permute-start(bf16[5,128,128]{2,1,0:T(8,128)(2,1)S(1)} %first_layer.2.rest_0_), channel_id=1, source_target_pairs={{0,1},{1,0},{2,3},{3,2},{4,5},{5,4},{6,7},{7,6},{8,9},{9,8},{10,11... | collective-permute-start | bytes 491528 | tf_op jit(solution)/shard_map/ppermute | solution.py:295
  25.4 8.0 %collective-permute-start.7 = (bf16[5,128,128]{2,1,0:T(8,128)(2,1)S(1)}, bf16[5,128,128]{2,1,0:T(8,128)(2,1)S(1)}, u32[]{:S(2)}, u32[]{:S(2)}) collective-permute-start(bf16[5,128,128]{2,1,0:T(8,128)(2,1)S(1)} %add_convert_fusion.own_ref), channel_id=1, source_target_pairs={{0,16},{2,18},{4,20},{6,22},{8,24},{10,26},{12,28},{14,30},{16,0},... | collective-permute-start | bytes 491528 | tf_op jit(solution)/shard_map/ppermute | solution.py:292
  33.4 5.4 %collective-permute-start.11 = (bf16[5,128,128]{2,1,0:T(8,128)(2,1)S(1)}, bf16[5,128,128]{2,1,0:T(8,128)(2,1)S(1)}, u32[]{:S(2)}, u32[]{:S(2)}) collective-permute-start(bf16[5,128,128]{2,1,0:T(8,128)(2,1)S(1)} %get-tuple-element.22), channel_id=1, source_target_pairs={{0,1},{1,0},{2,3},{3,2},{4,5},{5,4},{6,7},{7,6},{8,9},{9,8},{10,11... | collective-permute-start | bytes 491528 | tf_op jit(solution)/shard_map/ppermute | solution.py:295
  35.0 8.1 %collective-permute-start.10 = (bf16[5,128,128]{2,1,0:T(8,128)(2,1)S(1)}, bf16[5,128,128]{2,1,0:T(8,128)(2,1)S(1)}, u32[]{:S(2)}, u32[]{:S(2)}) collective-permute-start(bf16[5,128,128]{2,1,0:T(8,128)(2,1)S(1)} %get-tuple-element.21.refs_0_), channel_id=1, source_target_pairs={{0,12},{2,14},{4,8},{6,10},{8,4},{10,6},{12,0},{14,2},{16,28},{18,... | collective-permute-start | bytes 491528 | tf_op jit(solution)/shard_map/ppermute | solution.py:292
  35.0 10.8 %collective-permute-start.9 = (bf16[5,128,128]{2,1,0:T(8,128)(2,1)S(1)}, bf16[5,128,128]{2,1,0:T(8,128)(2,1)S(1)}, u32[]{:S(2)}, u32[]{:S(2)}) collective-permute-start(bf16[5,128,128]{2,1,0:T(8,128)(2,1)S(1)} %get-tuple-element.21.refs_0_), channel_id=1, source_target_pairs={{0,8},{2,10},{4,12},{6,14},{8,0},{10,2},{12,4},{14,6},{16,24},{18,... | collective-permute-start | bytes 491528 | tf_op jit(solution)/shard_map/ppermute | solution.py:292
  37.1 10.7 %collective-permute-start.8 = (bf16[5,128,128]{2,1,0:T(8,128)(2,1)S(1)}, bf16[5,128,128]{2,1,0:T(8,128)(2,1)S(1)}, u32[]{:S(2)}, u32[]{:S(2)}) collective-permute-start(bf16[5,128,128]{2,1,0:T(8,128)(2,1)S(1)} %get-tuple-element.21.refs_0_), channel_id=1, source_target_pairs={{0,4},{2,6},{4,0},{6,2},{8,12},{10,14},{12,8},{14,10},{16,20},{18,... | collective-permute-start | bytes 491528 | tf_op jit(solution)/shard_map/ppermute | solution.py:292
  38.8 10.5 %collective-permute-start.14 = (bf16[5,128,128]{2,1,0:T(8,128)(2,1)S(1)}, bf16[5,128,128]{2,1,0:T(8,128)(2,1)S(1)}, u32[]{:S(2)}, u32[]{:S(2)}) collective-permute-start(bf16[5,128,128]{2,1,0:T(8,128)(2,1)S(1)} %collective-permute-done.11.refs_0_), channel_id=1, source_target_pairs={{0,12},{2,14},{4,8},{6,10},{8,4},{10,6},{12,0},{14,2},{16,28},{18,... | collective-permute-start | bytes 491528 | tf_op jit(solution)/shard_map/ppermute | solution.py:292
  39.1 11.2 %collective-permute-start.13 = (bf16[5,128,128]{2,1,0:T(8,128)(2,1)S(1)}, bf16[5,128,128]{2,1,0:T(8,128)(2,1)S(1)}, u32[]{:S(2)}, u32[]{:S(2)}) collective-permute-start(bf16[5,128,128]{2,1,0:T(8,128)(2,1)S(1)} %collective-permute-done.11.refs_0_), channel_id=1, source_target_pairs={{0,8},{2,10},{4,12},{6,14},{8,0},{10,2},{12,4},{14,6},{16,24},{18,... | collective-permute-start | bytes 491528 | tf_op jit(solution)/shard_map/ppermute | solution.py:292
  43.1 7.8 %collective-permute-start.12 = (bf16[5,128,128]{2,1,0:T(8,128)(2,1)S(1)}, bf16[5,128,128]{2,1,0:T(8,128)(2,1)S(1)}, u32[]{:S(2)}, u32[]{:S(2)}) collective-permute-start(bf16[5,128,128]{2,1,0:T(8,128)(2,1)S(1)} %collective-permute-done.11.refs_0_), channel_id=1, source_target_pairs={{0,4},{2,6},{4,0},{6,2},{8,12},{10,14},{12,8},{14,10},{16,20},{18,... | collective-permute-start | bytes 491528 | tf_op jit(solution)/shard_map/ppermute | solution.py:292
  47.8 3.2 %collective-permute-start.15 = (bf16[20,128,128]{2,1,0:T(8,128)(2,1)S(1)}, bf16[20,128,128]{2,1,0:T(8,128)(2,1)S(1)}, u32[]{:S(2)}, u32[]{:S(2)}) collective-permute-start(bf16[20,128,128]{2,1,0:T(8,128)(2,1)S(1)} %own_joined.2.home_ref), channel_id=1, source_target_pairs={{0,2},{2,0},{4,6},{6,4},{8,10},{10,8},{12,14},{14,12},{16,18},{18,... | collective-permute-start | bytes 1966088 | tf_op jit(solution)/shard_map/ppermute | solution.py:292
  50.9 2.2 %collective-permute-start.16 = (bf16[20,128,128]{2,1,0:T(8,128)(2,1)S(1)}, bf16[20,128,128]{2,1,0:T(8,128)(2,1)S(1)}, u32[]{:S(2)}, u32[]{:S(2)}) collective-permute-start(bf16[20,128,128]{2,1,0:T(8,128)(2,1)S(1)} %own_joined.3.away_ref), channel_id=1, source_target_pairs={{0,2},{2,0},{4,6},{6,4},{8,10},{10,8},{12,14},{14,12},{16,18},{18,... | collective-permute-start | bytes 1966088 | tf_op jit(solution)/shard_map/ppermute | solution.py:292
  55.3 7.0 %collective-permute-start.18 = (bf16[5,128,128]{2,1,0:T(8,128)(2,1)S(1)}, bf16[5,128,128]{2,1,0:T(8,128)(2,1)S(1)}, u32[]{:S(2)}, u32[]{:S(2)}) collective-permute-start(bf16[5,128,128]{2,1,0:T(8,128)(2,1)S(1)} %get-tuple-element.24.mine_ref), channel_id=1, source_target_pairs={{0,1},{1,0},{2,3},{3,2},{4,5},{5,4},{6,7},{7,6},{8,9},{9,8},{10,11... | collective-permute-start | bytes 491528 | tf_op jit(solution)/shard_map/ppermute | solution.py:295
  58.2 6.3 %collective-permute-start.17 = (bf16[5,128,128]{2,1,0:T(8,128)(2,1)S(1)}, bf16[5,128,128]{2,1,0:T(8,128)(2,1)S(1)}, u32[]{:S(2)}, u32[]{:S(2)}) collective-permute-start(bf16[5,128,128]{2,1,0:T(8,128)(2,1)S(1)} %second_layer.3.mine_ref), channel_id=1, source_target_pairs={{0,1},{1,0},{2,3},{3,2},{4,5},{5,4},{6,7},{7,6},{8,9},{9,8},{10,11... | collective-permute-start | bytes 491528 | tf_op jit(solution)/shard_map/ppermute | solution.py:295

commit v2 on v1

--- a/solution.py
+++ b/solution.py
@@ -131,10 +131,9 @@
             coef_ref[row, slot] = scaled_block(row, slot, cols_ref, counts_ref, inverse_ref, blocks_ref)
 
     rows = [first_row(True, count) + b for b in range(count)]
-    for row in rows:
-        scale(row, first)
     def one_row(b, carry):
         row = rows[0] + b
+        scale(row, first)
         for part in others:
 
             @pl.when(counts_ref[row] > part.start)
@@ -143,8 +142,7 @@
 
         return carry
 
-    if others:
-        lax.fori_loop(0, len(rows), one_row, 0)
+    lax.fori_loop(0, len(rows), one_row, 0)
 
 
 def fetch_kernel(demand_hbm, _, demand_ref, sem):
@@ -217,7 +215,7 @@
     second_rows(0, lambda col: col, cols_ref, counts_ref, coef_ref, source_ref, start, out_ref, acc_ref)
 
 
-def choose_kernel(own_ref, crossed_ref, _, home_ref, away_ref):
+def choose_kernel(own_ref, crossed_ref, home_ref, away_ref):
     owner = lax.div(lax.axis_index("row"), 8) == lax.axis_index("col")
 
     @pl.when(owner)
@@ -232,7 +230,7 @@
 
 
 def join_kernel(*refs):
-    pieces, joined_ref = refs[:-1], refs[-1]
+    pieces, joined_ref = refs[:4], refs[-1]
     part = pieces[0].shape[0]
     for i, piece in enumerate(pieces):
         joined_ref[i * part : (i + 1) * part] = piece[...]
@@ -386,23 +384,26 @@
         choose_kernel,
         name="home_and_away",
         out_shape=(piece, piece),
-        in_specs=[VMEM] * 3,
+        in_specs=[VMEM] * 2,
         out_specs=(VMEM, VMEM),
         compiler_params=PARAMS,
-    )(own, flip(own, group_devices), token)
-
-    def join(pieces):
+    )(own, flip(own, group_devices))
+
+    def join(pieces, earlier):
         return pl.pallas_call(
             join_kernel,
             name="own_joined",
             out_shape=jax.ShapeDtypeStruct((len(pieces) * half, size, width), own.dtype),
-            in_specs=[VMEM] * len(pieces),
+            in_specs=[VMEM] * (len(pieces) + len(earlier)),
             out_specs=VMEM,
             compiler_params=PARAMS,
-        )(*pieces)
+        )(*pieces, *earlier)
 
     away = swap(away)
-    home, away = [join([part] + [flip(part, mask) for mask in (2, 4, 6)]) for part in (home, away)]
+    home, away = [
+        join([part] + [flip(part, mask) for mask in (2, 4, 6)], earlier)
+        for part, earlier in ((home, [token]), (away, []))
+    ]
     home_core, away_core = flip(home, 1), flip(away, 1)
     source = pl.pallas_call(
         collect_kernel,

time: 65.2 us -> 65.9 us (1.011)
  waiting for transfers between devices: 26.4 us -> 31.2 us
  Pallas kernels: 16.9 us -> 14.8 us
  starting transfers between devices: 21.6 us -> 20 us
    ppermute x15, waiting for transfers between devices: 20.9 us -> 24.4 us  [flip(): return lax.ppermute(array, 'row', [(i, i ^ mask) for i in range(n_row)])]
    ppermute x15, starting transfers between devices: 15.9 us -> 14.2 us  [flip(): return lax.ppermute(array, 'row', [(i, i ^ mask) for i in range(n_row)])]
    ppermute x4, waiting for transfers between devices: 5.44 us -> 6.79 us  [swap(): return lax.ppermute(array, 'col', [(0, 1), (1, 0)])]
    pallas_call x2, Pallas kernels: 4.58 us -> 3.83 us  [first_layer(): pl.pallas_call(functools.partial(first_kernel, sending), name='first_laye...]
    pallas_call x2, Pallas kernels: 4.05 us -> 3.31 us  [second_call(): pl.pallas_call(kernel, name='second_layer', out_shape=(out, pltpu.VMEM((g...]
  transfers between devices with their start and end apart: 19 -> 19, of which waited for: 15 -> 14; matrix products, arithmetic and copies ran while one was open for 0% -> 0% of each run, Pallas kernels for 13% -> 12%
where the time goes in v2:
time: 65.9 us; the launch traced here: 66.3 us
  waiting for transfers between devices  31.2 us (47%)
  starting transfers between devices  20 us (30%)
  Pallas kernels  14.8 us (22%)
    ppermute x15, waiting for transfers between devices, flip(): return lax.ppermute(array, 'row', [(i, i ^ mask) for i in range(n_row)])  24.4 us
    ppermute x15, starting transfers between devices, flip(): return lax.ppermute(array, 'row', [(i, i ^ mask) for i in range(n_row)])  14.2 us
    ppermute x4, waiting for transfers between devices, swap(): return lax.ppermute(array, 'col', [(0, 1), (1, 0)])  6.79 us
    ppermute x4, starting transfers between devices, swap(): return lax.ppermute(array, 'col', [(0, 1), (1, 0)])  5.78 us
    pallas_call x2, Pallas kernels, first_layer(): pl.pallas_call(functools.partial(first_kernel, sending), name='first_laye...  3.83 us
    pallas_call x2, Pallas kernels, second_call(): pl.pallas_call(kernel, name='second_layer', out_shape=(out, pltpu.VMEM((g...  3.31 us
    pallas_call x1, Pallas kernels, body(): pl.pallas_call(sums_kernel, name='column_sums', out_shape=(jax.ShapeDtype...  3.07 us
    pallas_call x1, Pallas kernels, body(): pl.pallas_call(fetch_kernel, name='own_demand', out_shape=pltpu.VMEM(dema...  1.75 us
  transfers between devices with their start and end apart: 19, of which 14 were waited for; matrix products, arithmetic and copies ran while one was open for 0% of the time, Pallas kernels for 12%

profile of v2, /device:TPU:0, one launch (start us, length us, event | category | flops | bytes accessed | tf_op | source)
XLA Modules:
  0.0 66.3 jit_solution(5896433121947742909)
XLA Ops:
  0.0 0.0 copy-start.1
  0.0 0.0 copy-start.2
  0.0 0.0 copy-start
  0.0 3.1 %column_sums.1 = (f32[80,128]{1,0:T(8,128)S(1)}, bf16[10,36,128,128]{3,2,1,0:T(8,128)(2,1)S(1)}) custom-call(s32[10,36]{1,0:T(8,128)} %cols_ref.9, s32[10]{0:T(128)} %bitcast.9, bf16[10,36,128,128]{3,2,1,0:T(8,128)(2,1)} %blocks_ref.1), custom_call_target="tpu_custom_call" | custom-call | bytes 23592960 | tf_op jit(solution)/shard_map/column_sums/pallas_call | solution.py:269
  3.1 3.0 %collective-permute-start.1 = (bf16[80,128]{1,0:T(8,128)(2,1)S(1)}, bf16[80,128]{1,0:T(8,128)(2,1)S(1)}, u32[]{:S(2)}, u32[]{:S(2)}) collective-permute-start(bf16[80,128]{1,0:T(8,128)(2,1)S(1)} %convert_element_type.36), channel_id=1, source_target_pairs={{0,4},{2,6},{4,0},{6,2},{8,12},{10,14},{12,8},{14,10},{16,20},{18,... | collective-permute-start | bytes 61448 | tf_op jit(solution)/shard_map/ppermute | solution.py:290
  6.1 0.0 collective-permute-start
  6.1 0.2 collective-permute-start.2
  6.3 1.6 %collective-permute-done.1 = bf16[80,128]{1,0:T(8,128)(2,1)S(1)} collective-permute-done((bf16[80,128]{1,0:T(8,128)(2,1)S(1)}, bf16[80,128]{1,0:T(8,128)(2,1)S(1)}, u32[]{:S(2)}, u32[]{:S(2)}) %collective-permute-start.1) | collective-permute-done | bytes 20512 | tf_op jit(solution)/shard_map/ppermute | solution.py:290
  7.9 0.0 collective-permute-done
  7.9 1.4 %collective-permute-done.2 = bf16[80,128]{1,0:T(8,128)(2,1)S(1)} collective-permute-done((bf16[80,128]{1,0:T(8,128)(2,1)S(1)}, bf16[80,128]{1,0:T(8,128)(2,1)S(1)}, u32[]{:S(2)}, u32[]{:S(2)}) %collective-permute-start.2) | collective-permute-done | bytes 20512 | tf_op jit(solution)/shard_map/ppermute | solution.py:290
  9.3 3.3 %collective-permute-start.5 = (bf16[80,128]{1,0:T(8,128)(2,1)S(1)}, bf16[80,128]{1,0:T(8,128)(2,1)S(1)}, u32[]{:S(2)}, u32[]{:S(2)}) collective-permute-start(bf16[80,128]{1,0:T(8,128)(2,1)S(1)} %add_convert_fusion.1._), channel_id=1, source_target_pairs={{0,16},{2,18},{4,20},{6,22},{8,24},{10,26},{12,28},{14,30},{16,0},... | collective-permute-start | bytes 61448 | tf_op jit(solution)/shard_map/ppermute | solution.py:290
  12.6 0.7 %collective-permute-start.4 = (bf16[80,128]{1,0:T(8,128)(2,1)S(1)}, bf16[80,128]{1,0:T(8,128)(2,1)S(1)}, u32[]{:S(2)}, u32[]{:S(2)}) collective-permute-start(bf16[80,128]{1,0:T(8,128)(2,1)S(1)} %add_convert_fusion.1._), channel_id=1, source_target_pairs={{0,24},{2,26},{4,28},{6,30},{8,16},{10,18},{12,20},{14,22},{16,8},... | collective-permute-start | bytes 61448 | tf_op jit(solution)/shard_map/ppermute | solution.py:290
  13.4 0.1 collective-permute-start.3
  13.5 1.7 %own_demand.1 = bf16[10240,128]{1,0:T(8,128)(2,1)S(1)} custom-call(bf16[10240,128]{1,0:T(8,128)(2,1)} %demand_hbm.1, bf16[80,128]{1,0:T(8,128)(2,1)S(1)} %add_convert_fusion.1._), custom_call_target="tpu_custom_call" | custom-call | bytes 7864320 | tf_op jit(solution)/shard_map/own_demand/pallas_call | solution.py:300
  15.2 0.0 collective-permute-done.5
  15.2 3.0 %collective-permute-done.4 = bf16[80,128]{1,0:T(8,128)(2,1)S(1)} collective-permute-done((bf16[80,128]{1,0:T(8,128)(2,1)S(1)}, bf16[80,128]{1,0:T(8,128)(2,1)S(1)}, u32[]{:S(2)}, u32[]{:S(2)}) %collective-permute-start.4) | collective-permute-done | bytes 20512 | tf_op jit(solution)/shard_map/ppermute | solution.py:290
  18.2 0.0 collective-permute-done.3
  18.2 0.0 copy-done.1
  18.3 0.0 copy-done.2
  18.3 0.0 copy-done
  18.3 1.5 %first_layer.2.rest_0_ = bf16[5,128,128]{2,1,0:T(8,128)(2,1)S(1)} custom-call(s32[10,36]{1,0:T(8,128)S(1)} %copy-done.1, s32[10]{0:T(128)S(1)} %bitcast.10, f32[80,128]{1,0:T(8,128)S(1)} %convert_add_fusion.sums_ref, f32[80,128]{1,0:T(8,128)S(1)} %bitcast.6, bf16[80,128,128]{2,1,0:T(8,128)(2,1)S(1)} %bitcast.4, ...), custom_call_target="tpu_custom_call" | custom-call | flops 754974720 | bytes 5898240 | tf_op jit(solution)/shard_map/first_layer/pallas_call | solution.py:319
  19.8 1.9 %collective-permute-start.6 = (bf16[5,128,128]{2,1,0:T(8,128)(2,1)S(1)}, bf16[5,128,128]{2,1,0:T(8,128)(2,1)S(1)}, u32[]{:S(2)}, u32[]{:S(2)}) collective-permute-start(bf16[5,128,128]{2,1,0:T(8,128)(2,1)S(1)} %first_layer.2.rest_0_), channel_id=1, source_target_pairs={{0,1},{1,0},{2,3},{3,2},{4,5},{5,4},{6,7},{7,6},{8,9},{9,8},{10,11... | collective-permute-start | bytes 491528 | tf_op jit(solution)/shard_map/ppermute | solution.py:293
  21.7 2.3 %first_layer.3 = (f32[5,128,128]{2,1,0:T(8,128)S(1)}, bf16[10,36,128,128]{3,2,1,0:T(8,128)(2,1)S(1)}) custom-call(s32[10,36]{1,0:T(8,128)S(1)} %copy-done.1, s32[10]{0:T(128)S(1)} %bitcast.11, f32[80,128]{1,0:T(8,128)S(1)} %convert_add_fusion.sums_ref, f32[80,128]{1,0:T(8,128)S(1)} %bitcast.7, ...), custom_call_target="tpu_custom_call", output_to_operand_aliasing={{1}: (5, {})} | custom-call | flops 754974720 | bytes 5898240 | tf_op jit(solution)/shard_map/first_layer/pallas_call | solution.py:319
  24.0 1.3 %collective-permute-done.6 = bf16[5,128,128]{2,1,0:T(8,128)(2,1)S(1)} collective-permute-done((bf16[5,128,128]{2,1,0:T(8,128)(2,1)S(1)}, bf16[5,128,128]{2,1,0:T(8,128)(2,1)S(1)}, u32[]{:S(2)}, u32[]{:S(2)}) %collective-permute-start.6) | collective-permute-done | bytes 163872 | tf_op jit(solution)/shard_map/ppermute | solution.py:293
  25.4 1.4 %collective-permute-start.7 = (bf16[5,128,128]{2,1,0:T(8,128)(2,1)S(1)}, bf16[5,128,128]{2,1,0:T(8,128)(2,1)S(1)}, u32[]{:S(2)}, u32[]{:S(2)}) collective-permute-start(bf16[5,128,128]{2,1,0:T(8,128)(2,1)S(1)} %add_convert_fusion.own_ref), channel_id=1, source_target_pairs={{0,16},{2,18},{4,20},{6,22},{8,24},{10,26},{12,28},{14,30},{16,0},... | collective-permute-start | bytes 491528 | tf_op jit(solution)/shard_map/ppermute | solution.py:290
  26.8 6.8 %collective-permute-done.7.crossed_ref = bf16[5,128,128]{2,1,0:T(8,128)(2,1)S(1)} collective-permute-done((bf16[5,128,128]{2,1,0:T(8,128)(2,1)S(1)}, bf16[5,128,128]{2,1,0:T(8,128)(2,1)S(1)}, u32[]{:S(2)}, u32[]{:S(2)}) %collective-permute-start.7) | collective-permute-done | bytes 163872 | tf_op jit(solution)/shard_map/ppermute | solution.py:290
  33.6 1.7 %collective-permute-start.11 = (bf16[5,128,128]{2,1,0:T(8,128)(2,1)S(1)}, bf16[5,128,128]{2,1,0:T(8,128)(2,1)S(1)}, u32[]{:S(2)}, u32[]{:S(2)}) collective-permute-start(bf16[5,128,128]{2,1,0:T(8,128)(2,1)S(1)} %get-tuple-element.22), channel_id=1, source_target_pairs={{0,1},{1,0},{2,3},{3,2},{4,5},{5,4},{6,7},{7,6},{8,9},{9,8},{10,11... | collective-permute-start | bytes 491528 | tf_op jit(solution)/shard_map/ppermute | solution.py:293
  35.3 0.0 collective-permute-start.10
  35.3 1.6 %collective-permute-start.9 = (bf16[5,128,128]{2,1,0:T(8,128)(2,1)S(1)}, bf16[5,128,128]{2,1,0:T(8,128)(2,1)S(1)}, u32[]{:S(2)}, u32[]{:S(2)}) collective-permute-start(bf16[5,128,128]{2,1,0:T(8,128)(2,1)S(1)} %get-tuple-element.20.refs_0_), channel_id=1, source_target_pairs={{0,8},{2,10},{4,12},{6,14},{8,0},{10,2},{12,4},{14,6},{16,24},{18,... | collective-permute-start | bytes 491528 | tf_op jit(solution)/shard_map/ppermute | solution.py:290
  36.9 1.9 %collective-permute-start.8 = (bf16[5,128,128]{2,1,0:T(8,128)(2,1)S(1)}, bf16[5,128,128]{2,1,0:T(8,128)(2,1)S(1)}, u32[]{:S(2)}, u32[]{:S(2)}) collective-permute-start(bf16[5,128,128]{2,1,0:T(8,128)(2,1)S(1)} %get-tuple-element.20.refs_0_), channel_id=1, source_target_pairs={{0,4},{2,6},{4,0},{6,2},{8,12},{10,14},{12,8},{14,10},{16,20},{18,... | collective-permute-start | bytes 491528 | tf_op jit(solution)/shard_map/ppermute | solution.py:290
  38.8 0.3 collective-permute-done.11.refs_0_
  39.1 0.0 collective-permute-start.14
  39.1 1.7 %collective-permute-start.13 = (bf16[5,128,128]{2,1,0:T(8,128)(2,1)S(1)}, bf16[5,128,128]{2,1,0:T(8,128)(2,1)S(1)}, u32[]{:S(2)}, u32[]{:S(2)}) collective-permute-start(bf16[5,128,128]{2,1,0:T(8,128)(2,1)S(1)} %collective-permute-done.11.refs_0_), channel_id=1, source_target_pairs={{0,8},{2,10},{4,12},{6,14},{8,0},{10,2},{12,4},{14,6},{16,24},{18,... | collective-permute-start | bytes 491528 | tf_op jit(solution)/shard_map/ppermute | solution.py:290
  40.8 2.5 %collective-permute-done.10.refs_3_ = bf16[5,128,128]{2,1,0:T(8,128)(2,1)S(1)} collective-permute-done((bf16[5,128,128]{2,1,0:T(8,128)(2,1)S(1)}, bf16[5,128,128]{2,1,0:T(8,128)(2,1)S(1)}, u32[]{:S(2)}, u32[]{:S(2)}) %collective-permute-start.10) | collective-permute-done | bytes 163872 | tf_op jit(solution)/shard_map/ppermute | solution.py:290
  43.3 0.2 collective-permute-start.12
  43.5 1.2 %own_coefficients.1 = (bf16[10,36,128,128]{3,2,1,0:T(8,128)(2,1)S(1)}, f32[8,128]{1,0:T(8,128)S(1)}) custom-call(s32[10,36]{1,0:T(8,128)S(1)} %copy-done.1, s32[10]{0:T(128)S(1)} %bitcast.12, f32[80,128]{1,0:T(8,128)S(1)} %convert_add_fusion.sums_ref, f32[80,128]{1,0:T(8,128)S(1)} %bitcast.8, ...), custom_call_target="tpu_custom_call", output_to_operand_aliasing={{0}: (4, {})} | custom-call | flops 754974720 | bytes 5898240 | tf_op jit(solution)/shard_map/own_coefficients/pallas_call | solution.py:369
  44.7 0.8 %collective-permute-done.9.refs_2_ = bf16[5,128,128]{2,1,0:T(8,128)(2,1)S(1)} collective-permute-done((bf16[5,128,128]{2,1,0:T(8,128)(2,1)S(1)}, bf16[5,128,128]{2,1,0:T(8,128)(2,1)S(1)}, u32[]{:S(2)}, u32[]{:S(2)}) %collective-permute-start.9) | collective-permute-done | bytes 163872 | tf_op jit(solution)/shard_map/ppermute | solution.py:290
  45.5 2.0 %collective-permute-done.8.refs_1_ = bf16[5,128,128]{2,1,0:T(8,128)(2,1)S(1)} collective-permute-done((bf16[5,128,128]{2,1,0:T(8,128)(2,1)S(1)}, bf16[5,128,128]{2,1,0:T(8,128)(2,1)S(1)}, u32[]{:S(2)}, u32[]{:S(2)}) %collective-permute-start.8) | collective-permute-done | bytes 163872 | tf_op jit(solution)/shard_map/ppermute | solution.py:290
  47.6 0.1 collective-permute-start.15
  47.7 2.6 %collective-permute-done.14.refs_3_ = bf16[5,128,128]{2,1,0:T(8,128)(2,1)S(1)} collective-permute-done((bf16[5,128,128]{2,1,0:T(8,128)(2,1)S(1)}, bf16[5,128,128]{2,1,0:T(8,128)(2,1)S(1)}, u32[]{:S(2)}, u32[]{:S(2)}) %collective-permute-start.14) | collective-permute-done | bytes 163872 | tf_op jit(solution)/shard_map/ppermute | solution.py:290
  50.3 0.0 collective-permute-done.13.refs_2_
  50.3 1.7 %collective-permute-done.12.refs_1_ = bf16[5,128,128]{2,1,0:T(8,128)(2,1)S(1)} collective-permute-done((bf16[5,128,128]{2,1,0:T(8,128)(2,1)S(1)}, bf16[5,128,128]{2,1,0:T(8,128)(2,1)S(1)}, u32[]{:S(2)}, u32[]{:S(2)}) %collective-permute-start.12) | collective-permute-done | bytes 163872 | tf_op jit(solution)/shard_map/ppermute | solution.py:290
  52.1 0.1 collective-permute-start.16
  52.1 0.0 collective-permute-done.15.home_core_ref
  52.2 0.1 own_collected.1.rest_0_
  52.3 1.9 %collective-permute-done.16.rest_1_ = bf16[20,128,128]{2,1,0:T(8,128)(2,1)S(1)} collective-permute-done((bf16[20,128,128]{2,1,0:T(8,128)(2,1)S(1)}, bf16[20,128,128]{2,1,0:T(8,128)(2,1)S(1)}, u32[]{:S(2)}, u32[]{:S(2)}) %collective-permute-start.16) | collective-permute-done | bytes 655392 | tf_op jit(solution)/shard_map/ppermute | solution.py:290
  54.2 1.9 %second_layer.2 = (bf16[5,128,128]{2,1,0:T(8,128)(2,1)S(1)}, bf16[80,128,128]{2,1,0:T(8,128)(2,1)S(1)}) custom-call(s32[10,36]{1,0:T(8,128)S(1)} %copy-done.1, s32[10]{0:T(128)S(1)} %bitcast.13, bf16[10,36,128,128]{3,2,1,0:T(8,128)(2,1)S(1)} %get-tuple-element.18.coef_ref, ...), custom_call_target="tpu_custom_call", output_to_operand_aliasing={{1}: (4, {})} | custom-call | flops 754974720 | bytes 5898240 | tf_op jit(solution)/shard_map/second_layer/pallas_call | solution.py:345
  56.1 0.4 collective-permute-start.18
  56.5 1.4 %second_layer.3.mine_ref = bf16[5,128,128]{2,1,0:T(8,128)(2,1)S(1)} custom-call(s32[10,36]{1,0:T(8,128)S(1)} %copy-done.1, s32[10]{0:T(128)S(1)} %bitcast.14, bf16[10,36,128,128]{3,2,1,0:T(8,128)(2,1)S(1)} %get-tuple-element.18.coef_ref, bf16[5,128,128]{2,1,0:T(8,128)(2,1)S(1)} %add_convert_fusion.own_ref, bf16[80,128,128]{2,1,0:T(8,128)(2,1)S(1)} %get-tuple-element.23.rest_0_), custom_call_target="tpu_custom_call" | custom-call | flops 754974720 | bytes 5898240 | tf_op jit(solution)/shard_map/second_layer/pallas_call | solution.py:345
  58.0 1.7 %collective-permute-start.17 = (bf16[5,128,128]{2,1,0:T(8,128)(2,1)S(1)}, bf16[5,128,128]{2,1,0:T(8,128)(2,1)S(1)}, u32[]{:S(2)}, u32[]{:S(2)}) collective-permute-start(bf16[5,128,128]{2,1,0:T(8,128)(2,1)S(1)} %second_layer.3.mine_ref), channel_id=1, source_target_pairs={{0,1},{1,0},{2,3},{3,2},{4,5},{5,4},{6,7},{7,6},{8,9},{9,8},{10,11... | collective-permute-start | bytes 491528 | tf_op jit(solution)/shard_map/ppermute | solution.py:293
  59.7 3.5 %collective-permute-done.18.other_ref = bf16[5,128,128]{2,1,0:T(8,128)(2,1)S(1)} collective-permute-done((bf16[5,128,128]{2,1,0:T(8,128)(2,1)S(1)}, bf16[5,128,128]{2,1,0:T(8,128)(2,1)S(1)}, u32[]{:S(2)}, u32[]{:S(2)}) %collective-permute-start.18) | collective-permute-done | bytes 163872 | tf_op jit(solution)/shard_map/ppermute | solution.py:293
  63.3 0.7 %result.2.rest_0_ = bf16[10,128,128]{2,1,0:T(8,128)(2,1)} custom-call(bf16[5,128,128]{2,1,0:T(8,128)(2,1)S(1)} %get-tuple-element.24.mine_ref, bf16[5,128,128]{2,1,0:T(8,128)(2,1)S(1)} %collective-permute-done.18.other_ref), custom_call_target="tpu_custom_call" | custom-call | tf_op jit(solution)/shard_map/result/pallas_call | solution.py:426
  64.0 1.6 %collective-permute-done.17.other_ref = bf16[5,128,128]{2,1,0:T(8,128)(2,1)S(1)} collective-permute-done((bf16[5,128,128]{2,1,0:T(8,128)(2,1)S(1)}, bf16[5,128,128]{2,1,0:T(8,128)(2,1)S(1)}, u32[]{:S(2)}, u32[]{:S(2)}) %collective-permute-start.17) | collective-permute-done | bytes 163872 | tf_op jit(solution)/shard_map/ppermute | solution.py:293
  65.5 0.7 %result.3 = bf16[10,128,128]{2,1,0:T(8,128)(2,1)} custom-call(bf16[5,128,128]{2,1,0:T(8,128)(2,1)S(1)} %second_layer.3.mine_ref, bf16[5,128,128]{2,1,0:T(8,128)(2,1)S(1)} %collective-permute-done.17.other_ref, bf16[10,128,128]{2,1,0:T(8,128)(2,1)} %result.2.rest_0_), custom_call_target="tpu_custom_call", output_to_operand_aliasing={{}: (2, {})} | custom-call | tf_op jit(solution)/shard_map/result/pallas_call | solution.py:426
  (7 shorter events, 0.2 us)
Async XLA Ops:
  0.0 18.2 %copy-start.1 = (s32[10,36]{1,0:T(8,128)S(1)}, s32[10,36]{1,0:T(8,128)}, u32[]{:S(2)}) copy-start(s32[10,36]{1,0:T(8,128)} %cols_ref.9) | copy-start | bytes 4324
  0.0 18.3 %copy-start.2 = (s32[10,1]{0,1:T(1,128)S(1)}, s32[10,1]{0,1:T(1,128)}, u32[]{:S(2)}) copy-start(s32[10,1]{0,1:T(1,128)} %param.7) | copy-start | bytes 124
  0.0 18.3 %copy-start = (f32[10240]{0:T(1024)S(1)}, f32[10240]{0:T(1024)}, u32[]{:S(2)}) copy-start(f32[10240]{0:T(1024)} %param.9) | copy-start | bytes 122884
  3.1 4.8 %collective-permute-start.1 = (bf16[80,128]{1,0:T(8,128)(2,1)S(1)}, bf16[80,128]{1,0:T(8,128)(2,1)S(1)}, u32[]{:S(2)}, u32[]{:S(2)}) collective-permute-start(bf16[80,128]{1,0:T(8,128)(2,1)S(1)} %convert_element_type.36), channel_id=1, source_target_pairs={{0,4},{2,6},{4,0},{6,2},{8,12},{10,14},{12,8},{14,10},{16,20},{18,... | collective-permute-start | bytes 61448 | tf_op jit(solution)/shard_map/ppermute | solution.py:290
  6.1 1.8 %collective-permute-start = (bf16[80,128]{1,0:T(8,128)(2,1)S(1)}, bf16[80,128]{1,0:T(8,128)(2,1)S(1)}, u32[]{:S(2)}, u32[]{:S(2)}) collective-permute-start(bf16[80,128]{1,0:T(8,128)(2,1)S(1)} %convert_element_type.36), channel_id=1, source_target_pairs={{0,2},{2,0},{4,6},{6,4},{8,10},{10,8},{12,14},{14,12},{16,18},{18,... | collective-permute-start | bytes 61448 | tf_op jit(solution)/shard_map/ppermute | solution.py:290
  6.1 3.2 %collective-permute-start.2 = (bf16[80,128]{1,0:T(8,128)(2,1)S(1)}, bf16[80,128]{1,0:T(8,128)(2,1)S(1)}, u32[]{:S(2)}, u32[]{:S(2)}) collective-permute-start(bf16[80,128]{1,0:T(8,128)(2,1)S(1)} %convert_element_type.36), channel_id=1, source_target_pairs={{0,6},{2,4},{4,2},{6,0},{8,14},{10,12},{12,10},{14,8},{16,22},{18,... | collective-permute-start | bytes 61448 | tf_op jit(solution)/shard_map/ppermute | solution.py:290
  9.3 5.9 %collective-permute-start.5 = (bf16[80,128]{1,0:T(8,128)(2,1)S(1)}, bf16[80,128]{1,0:T(8,128)(2,1)S(1)}, u32[]{:S(2)}, u32[]{:S(2)}) collective-permute-start(bf16[80,128]{1,0:T(8,128)(2,1)S(1)} %add_convert_fusion.1._), channel_id=1, source_target_pairs={{0,16},{2,18},{4,20},{6,22},{8,24},{10,26},{12,28},{14,30},{16,0},... | collective-permute-start | bytes 61448 | tf_op jit(solution)/shard_map/ppermute | solution.py:290
  12.6 5.6 %collective-permute-start.4 = (bf16[80,128]{1,0:T(8,128)(2,1)S(1)}, bf16[80,128]{1,0:T(8,128)(2,1)S(1)}, u32[]{:S(2)}, u32[]{:S(2)}) collective-permute-start(bf16[80,128]{1,0:T(8,128)(2,1)S(1)} %add_convert_fusion.1._), channel_id=1, source_target_pairs={{0,24},{2,26},{4,28},{6,30},{8,16},{10,18},{12,20},{14,22},{16,8},... | collective-permute-start | bytes 61448 | tf_op jit(solution)/shard_map/ppermute | solution.py:290
  13.4 4.9 %collective-permute-start.3 = (bf16[80,128]{1,0:T(8,128)(2,1)S(1)}, bf16[80,128]{1,0:T(8,128)(2,1)S(1)}, u32[]{:S(2)}, u32[]{:S(2)}) collective-permute-start(bf16[80,128]{1,0:T(8,128)(2,1)S(1)} %add_convert_fusion.1._), channel_id=1, source_target_pairs={{0,8},{2,10},{4,12},{6,14},{8,0},{10,2},{12,4},{14,6},{16,24},{18,... | collective-permute-start | bytes 61448 | tf_op jit(solution)/shard_map/ppermute | solution.py:290
  19.8 5.6 %collective-permute-start.6 = (bf16[5,128,128]{2,1,0:T(8,128)(2,1)S(1)}, bf16[5,128,128]{2,1,0:T(8,128)(2,1)S(1)}, u32[]{:S(2)}, u32[]{:S(2)}) collective-permute-start(bf16[5,128,128]{2,1,0:T(8,128)(2,1)S(1)} %first_layer.2.rest_0_), channel_id=1, source_target_pairs={{0,1},{1,0},{2,3},{3,2},{4,5},{5,4},{6,7},{7,6},{8,9},{9,8},{10,11... | collective-permute-start | bytes 491528 | tf_op jit(solution)/shard_map/ppermute | solution.py:293
  25.4 8.1 %collective-permute-start.7 = (bf16[5,128,128]{2,1,0:T(8,128)(2,1)S(1)}, bf16[5,128,128]{2,1,0:T(8,128)(2,1)S(1)}, u32[]{:S(2)}, u32[]{:S(2)}) collective-permute-start(bf16[5,128,128]{2,1,0:T(8,128)(2,1)S(1)} %add_convert_fusion.own_ref), channel_id=1, source_target_pairs={{0,16},{2,18},{4,20},{6,22},{8,24},{10,26},{12,28},{14,30},{16,0},... | collective-permute-start | bytes 491528 | tf_op jit(solution)/shard_map/ppermute | solution.py:290
  33.6 5.5 %collective-permute-start.11 = (bf16[5,128,128]{2,1,0:T(8,128)(2,1)S(1)}, bf16[5,128,128]{2,1,0:T(8,128)(2,1)S(1)}, u32[]{:S(2)}, u32[]{:S(2)}) collective-permute-start(bf16[5,128,128]{2,1,0:T(8,128)(2,1)S(1)} %get-tuple-element.22), channel_id=1, source_target_pairs={{0,1},{1,0},{2,3},{3,2},{4,5},{5,4},{6,7},{7,6},{8,9},{9,8},{10,11... | collective-permute-start | bytes 491528 | tf_op jit(solution)/shard_map/ppermute | solution.py:293
  35.3 8.1 %collective-permute-start.10 = (bf16[5,128,128]{2,1,0:T(8,128)(2,1)S(1)}, bf16[5,128,128]{2,1,0:T(8,128)(2,1)S(1)}, u32[]{:S(2)}, u32[]{:S(2)}) collective-permute-start(bf16[5,128,128]{2,1,0:T(8,128)(2,1)S(1)} %get-tuple-element.20.refs_0_), channel_id=1, source_target_pairs={{0,12},{2,14},{4,8},{6,10},{8,4},{10,6},{12,0},{14,2},{16,28},{18,... | collective-permute-start | bytes 491528 | tf_op jit(solution)/shard_map/ppermute | solution.py:290
  35.3 10.2 %collective-permute-start.9 = (bf16[5,128,128]{2,1,0:T(8,128)(2,1)S(1)}, bf16[5,128,128]{2,1,0:T(8,128)(2,1)S(1)}, u32[]{:S(2)}, u32[]{:S(2)}) collective-permute-start(bf16[5,128,128]{2,1,0:T(8,128)(2,1)S(1)} %get-tuple-element.20.refs_0_), channel_id=1, source_target_pairs={{0,8},{2,10},{4,12},{6,14},{8,0},{10,2},{12,4},{14,6},{16,24},{18,... | collective-permute-start | bytes 491528 | tf_op jit(solution)/shard_map/ppermute | solution.py:290
  36.9 10.7 %collective-permute-start.8 = (bf16[5,128,128]{2,1,0:T(8,128)(2,1)S(1)}, bf16[5,128,128]{2,1,0:T(8,128)(2,1)S(1)}, u32[]{:S(2)}, u32[]{:S(2)}) collective-permute-start(bf16[5,128,128]{2,1,0:T(8,128)(2,1)S(1)} %get-tuple-element.20.refs_0_), channel_id=1, source_target_pairs={{0,4},{2,6},{4,0},{6,2},{8,12},{10,14},{12,8},{14,10},{16,20},{18,... | collective-permute-start | bytes 491528 | tf_op jit(solution)/shard_map/ppermute | solution.py:290
  39.1 11.1 %collective-permute-start.14 = (bf16[5,128,128]{2,1,0:T(8,128)(2,1)S(1)}, bf16[5,128,128]{2,1,0:T(8,128)(2,1)S(1)}, u32[]{:S(2)}, u32[]{:S(2)}) collective-permute-start(bf16[5,128,128]{2,1,0:T(8,128)(2,1)S(1)} %collective-permute-done.11.refs_0_), channel_id=1, source_target_pairs={{0,12},{2,14},{4,8},{6,10},{8,4},{10,6},{12,0},{14,2},{16,28},{18,... | collective-permute-start | bytes 491528 | tf_op jit(solution)/shard_map/ppermute | solution.py:290
  39.1 11.1 %collective-permute-start.13 = (bf16[5,128,128]{2,1,0:T(8,128)(2,1)S(1)}, bf16[5,128,128]{2,1,0:T(8,128)(2,1)S(1)}, u32[]{:S(2)}, u32[]{:S(2)}) collective-permute-start(bf16[5,128,128]{2,1,0:T(8,128)(2,1)S(1)} %collective-permute-done.11.refs_0_), channel_id=1, source_target_pairs={{0,8},{2,10},{4,12},{6,14},{8,0},{10,2},{12,4},{14,6},{16,24},{18,... | collective-permute-start | bytes 491528 | tf_op jit(solution)/shard_map/ppermute | solution.py:290
  43.3 8.7 %collective-permute-start.12 = (bf16[5,128,128]{2,1,0:T(8,128)(2,1)S(1)}, bf16[5,128,128]{2,1,0:T(8,128)(2,1)S(1)}, u32[]{:S(2)}, u32[]{:S(2)}) collective-permute-start(bf16[5,128,128]{2,1,0:T(8,128)(2,1)S(1)} %collective-permute-done.11.refs_0_), channel_id=1, source_target_pairs={{0,4},{2,6},{4,0},{6,2},{8,12},{10,14},{12,8},{14,10},{16,20},{18,... | collective-permute-start | bytes 491528 | tf_op jit(solution)/shard_map/ppermute | solution.py:290
  47.6 4.5 %collective-permute-start.15 = (bf16[20,128,128]{2,1,0:T(8,128)(2,1)S(1)}, bf16[20,128,128]{2,1,0:T(8,128)(2,1)S(1)}, u32[]{:S(2)}, u32[]{:S(2)}) collective-permute-start(bf16[20,128,128]{2,1,0:T(8,128)(2,1)S(1)} %own_joined.2.home_ref), channel_id=1, source_target_pairs={{0,2},{2,0},{4,6},{6,4},{8,10},{10,8},{12,14},{14,12},{16,18},{18,... | collective-permute-start | bytes 1966088 | tf_op jit(solution)/shard_map/ppermute | solution.py:290
  52.1 2.2 %collective-permute-start.16 = (bf16[20,128,128]{2,1,0:T(8,128)(2,1)S(1)}, bf16[20,128,128]{2,1,0:T(8,128)(2,1)S(1)}, u32[]{:S(2)}, u32[]{:S(2)}) collective-permute-start(bf16[20,128,128]{2,1,0:T(8,128)(2,1)S(1)} %own_joined.3.away_ref), channel_id=1, source_target_pairs={{0,2},{2,0},{4,6},{6,4},{8,10},{10,8},{12,14},{14,12},{16,18},{18,... | collective-permute-start | bytes 1966088 | tf_op jit(solution)/shard_map/ppermute | solution.py:290
  56.1 7.2 %collective-permute-start.18 = (bf16[5,128,128]{2,1,0:T(8,128)(2,1)S(1)}, bf16[5,128,128]{2,1,0:T(8,128)(2,1)S(1)}, u32[]{:S(2)}, u32[]{:S(2)}) collective-permute-start(bf16[5,128,128]{2,1,0:T(8,128)(2,1)S(1)} %get-tuple-element.24.mine_ref), channel_id=1, source_target_pairs={{0,1},{1,0},{2,3},{3,2},{4,5},{5,4},{6,7},{7,6},{8,9},{9,8},{10,11... | collective-permute-start | bytes 491528 | tf_op jit(solution)/shard_map/ppermute | solution.py:293
  58.0 7.6 %collective-permute-start.17 = (bf16[5,128,128]{2,1,0:T(8,128)(2,1)S(1)}, bf16[5,128,128]{2,1,0:T(8,128)(2,1)S(1)}, u32[]{:S(2)}, u32[]{:S(2)}) collective-permute-start(bf16[5,128,128]{2,1,0:T(8,128)(2,1)S(1)} %second_layer.3.mine_ref), channel_id=1, source_target_pairs={{0,1},{1,0},{2,3},{3,2},{4,5},{5,4},{6,7},{7,6},{8,9},{9,8},{10,11... | collective-permute-start | bytes 491528 | tf_op jit(solution)/shard_map/ppermute | solution.py:293

commit v3 on v1

--- a/solution.py
+++ b/solution.py
@@ -131,10 +131,10 @@
             coef_ref[row, slot] = scaled_block(row, slot, cols_ref, counts_ref, inverse_ref, blocks_ref)
 
     rows = [first_row(True, count) + b for b in range(count)]
-    for row in rows:
-        scale(row, first)
+
     def one_row(b, carry):
         row = rows[0] + b
+        scale(row, first)
         for part in others:
 
             @pl.when(counts_ref[row] > part.start)
@@ -143,8 +143,7 @@
 
         return carry
 
-    if others:
-        lax.fori_loop(0, len(rows), one_row, 0)
+    lax.fori_loop(0, len(rows), one_row, 0)
 
 
 def fetch_kernel(demand_hbm, _, demand_ref, sem):

time: 65.2 us -> 66.1 us (1.014); the launches traced: 65.1 us -> 64.9 us
  waiting for transfers between devices: 26.4 us -> 28.5 us
  starting transfers between devices: 21.6 us -> 20.1 us
  Pallas kernels: 16.9 us -> 15.9 us
    ppermute x4, waiting for transfers between devices: 5.44 us -> 7.15 us  [swap(): return lax.ppermute(array, 'col', [(0, 1), (1, 0)])]
    ppermute x4, starting transfers between devices: 5.63 us -> 4.75 us  [swap(): return lax.ppermute(array, 'col', [(0, 1), (1, 0)])]
where the time goes in v3:
time: 66.1 us; the launch traced here: 64.9 us
  waiting for transfers between devices  28.5 us (43%)
  starting transfers between devices  20.1 us (30%)
  Pallas kernels  15.9 us (24%)
    ppermute x15, waiting for transfers between devices, flip(): return lax.ppermute(array, 'row', [(i, i ^ mask) for i in range(n_row)])  21.4 us
    ppermute x15, starting transfers between devices, flip(): return lax.ppermute(array, 'row', [(i, i ^ mask) for i in range(n_row)])  15.4 us
    ppermute x4, waiting for transfers between devices, swap(): return lax.ppermute(array, 'col', [(0, 1), (1, 0)])  7.15 us
    ppermute x4, starting transfers between devices, swap(): return lax.ppermute(array, 'col', [(0, 1), (1, 0)])  4.75 us
    pallas_call x2, Pallas kernels, first_layer(): pl.pallas_call(functools.partial(first_kernel, sending), name='first_laye...  4.21 us
    pallas_call x2, Pallas kernels, second_call(): pl.pallas_call(kernel, name='second_layer', out_shape=(out, pltpu.VMEM((g...  3.68 us
    pallas_call x1, Pallas kernels, body(): pl.pallas_call(sums_kernel, name='column_sums', out_shape=(jax.ShapeDtype...  3.25 us
    pallas_call x1, Pallas kernels, body(): pl.pallas_call(fetch_kernel, name='own_demand', out_shape=pltpu.VMEM(dema...  1.75 us
  transfers between devices with their start and end apart: 19, of which 15 were waited for; matrix products, arithmetic and copies ran while one was open for 0% of the time, Pallas kernels for 13%

profile of v3, /device:TPU:0, one launch (start us, length us, event | category | flops | bytes accessed | tf_op | source)
XLA Modules:
  0.0 64.9 jit_solution(2223795498474544121)
XLA Ops:
  0.0 0.0 copy-start.1
  0.0 0.0 copy-start.2
  0.0 0.0 copy-start
  0.0 3.3 %column_sums.1 = (f32[80,128]{1,0:T(8,128)S(1)}, bf16[10,36,128,128]{3,2,1,0:T(8,128)(2,1)S(1)}) custom-call(s32[10,36]{1,0:T(8,128)} %cols_ref.9, s32[10]{0:T(128)} %bitcast.9, bf16[10,36,128,128]{3,2,1,0:T(8,128)(2,1)} %blocks_ref.1), custom_call_target="tpu_custom_call" | custom-call | bytes 23592960 | tf_op jit(solution)/shard_map/column_sums/pallas_call | solution.py:270
  3.3 3.1 %collective-permute-start.1 = (bf16[80,128]{1,0:T(8,128)(2,1)S(1)}, bf16[80,128]{1,0:T(8,128)(2,1)S(1)}, u32[]{:S(2)}, u32[]{:S(2)}) collective-permute-start(bf16[80,128]{1,0:T(8,128)(2,1)S(1)} %convert_element_type.36), channel_id=1, source_target_pairs={{0,4},{2,6},{4,0},{6,2},{8,12},{10,14},{12,8},{14,10},{16,20},{18,... | collective-permute-start | bytes 61448 | tf_op jit(solution)/shard_map/ppermute | solution.py:291
  6.3 0.0 collective-permute-start
  6.3 0.2 collective-permute-start.2
  6.5 1.6 %collective-permute-done.1 = bf16[80,128]{1,0:T(8,128)(2,1)S(1)} collective-permute-done((bf16[80,128]{1,0:T(8,128)(2,1)S(1)}, bf16[80,128]{1,0:T(8,128)(2,1)S(1)}, u32[]{:S(2)}, u32[]{:S(2)}) %collective-permute-start.1) | collective-permute-done | bytes 20512 | tf_op jit(solution)/shard_map/ppermute | solution.py:291
  8.1 0.0 collective-permute-done
  8.1 1.4 %collective-permute-done.2 = bf16[80,128]{1,0:T(8,128)(2,1)S(1)} collective-permute-done((bf16[80,128]{1,0:T(8,128)(2,1)S(1)}, bf16[80,128]{1,0:T(8,128)(2,1)S(1)}, u32[]{:S(2)}, u32[]{:S(2)}) %collective-permute-start.2) | collective-permute-done | bytes 20512 | tf_op jit(solution)/shard_map/ppermute | solution.py:291
  9.6 2.6 %collective-permute-start.5 = (bf16[80,128]{1,0:T(8,128)(2,1)S(1)}, bf16[80,128]{1,0:T(8,128)(2,1)S(1)}, u32[]{:S(2)}, u32[]{:S(2)}) collective-permute-start(bf16[80,128]{1,0:T(8,128)(2,1)S(1)} %add_convert_fusion.1._), channel_id=1, source_target_pairs={{0,16},{2,18},{4,20},{6,22},{8,24},{10,26},{12,28},{14,30},{16,0},... | collective-permute-start | bytes 61448 | tf_op jit(solution)/shard_map/ppermute | solution.py:291
  12.2 1.6 %collective-permute-start.4 = (bf16[80,128]{1,0:T(8,128)(2,1)S(1)}, bf16[80,128]{1,0:T(8,128)(2,1)S(1)}, u32[]{:S(2)}, u32[]{:S(2)}) collective-permute-start(bf16[80,128]{1,0:T(8,128)(2,1)S(1)} %add_convert_fusion.1._), channel_id=1, source_target_pairs={{0,24},{2,26},{4,28},{6,30},{8,16},{10,18},{12,20},{14,22},{16,8},... | collective-permute-start | bytes 61448 | tf_op jit(solution)/shard_map/ppermute | solution.py:291
  13.8 0.0 collective-permute-start.3
  13.8 1.7 %own_demand.1 = bf16[10240,128]{1,0:T(8,128)(2,1)S(1)} custom-call(bf16[10240,128]{1,0:T(8,128)(2,1)} %demand_hbm.1, bf16[80,128]{1,0:T(8,128)(2,1)S(1)} %add_convert_fusion.1._), custom_call_target="tpu_custom_call" | custom-call | bytes 7864320 | tf_op jit(solution)/shard_map/own_demand/pallas_call | solution.py:301
  15.5 0.0 collective-permute-done.5
  15.5 2.2 %collective-permute-done.4 = bf16[80,128]{1,0:T(8,128)(2,1)S(1)} collective-permute-done((bf16[80,128]{1,0:T(8,128)(2,1)S(1)}, bf16[80,128]{1,0:T(8,128)(2,1)S(1)}, u32[]{:S(2)}, u32[]{:S(2)}) %collective-permute-start.4) | collective-permute-done | bytes 20512 | tf_op jit(solution)/shard_map/ppermute | solution.py:291
  17.8 0.0 collective-permute-done.3
  17.8 0.0 copy-done.1
  17.8 0.0 copy-done.2
  17.8 0.0 copy-done
  17.8 1.9 %first_layer.2.rest_0_ = bf16[5,128,128]{2,1,0:T(8,128)(2,1)S(1)} custom-call(s32[10,36]{1,0:T(8,128)S(1)} %copy-done.1, s32[10]{0:T(128)S(1)} %bitcast.10, f32[80,128]{1,0:T(8,128)S(1)} %convert_add_fusion.sums_ref, f32[80,128]{1,0:T(8,128)S(1)} %bitcast.6, bf16[80,128,128]{2,1,0:T(8,128)(2,1)S(1)} %bitcast.4, ...), custom_call_target="tpu_custom_call" | custom-call | flops 754974720 | bytes 5898240 | tf_op jit(solution)/shard_map/first_layer/pallas_call | solution.py:320
  19.7 1.6 %collective-permute-start.6 = (bf16[5,128,128]{2,1,0:T(8,128)(2,1)S(1)}, bf16[5,128,128]{2,1,0:T(8,128)(2,1)S(1)}, u32[]{:S(2)}, u32[]{:S(2)}) collective-permute-start(bf16[5,128,128]{2,1,0:T(8,128)(2,1)S(1)} %first_layer.2.rest_0_), channel_id=1, source_target_pairs={{0,1},{1,0},{2,3},{3,2},{4,5},{5,4},{6,7},{7,6},{8,9},{9,8},{10,11... | collective-permute-start | bytes 491528 | tf_op jit(solution)/shard_map/ppermute | solution.py:294
  21.2 2.4 %first_layer.3 = (f32[5,128,128]{2,1,0:T(8,128)S(1)}, bf16[10,36,128,128]{3,2,1,0:T(8,128)(2,1)S(1)}) custom-call(s32[10,36]{1,0:T(8,128)S(1)} %copy-done.1, s32[10]{0:T(128)S(1)} %bitcast.11, f32[80,128]{1,0:T(8,128)S(1)} %convert_add_fusion.sums_ref, f32[80,128]{1,0:T(8,128)S(1)} %bitcast.7, ...), custom_call_target="tpu_custom_call", output_to_operand_aliasing={{1}: (5, {})} | custom-call | flops 754974720 | bytes 5898240 | tf_op jit(solution)/shard_map/first_layer/pallas_call | solution.py:320
  23.6 1.5 %collective-permute-done.6 = bf16[5,128,128]{2,1,0:T(8,128)(2,1)S(1)} collective-permute-done((bf16[5,128,128]{2,1,0:T(8,128)(2,1)S(1)}, bf16[5,128,128]{2,1,0:T(8,128)(2,1)S(1)}, u32[]{:S(2)}, u32[]{:S(2)}) %collective-permute-start.6) | collective-permute-done | bytes 163872 | tf_op jit(solution)/shard_map/ppermute | solution.py:294
  25.1 1.6 %collective-permute-start.7 = (bf16[5,128,128]{2,1,0:T(8,128)(2,1)S(1)}, bf16[5,128,128]{2,1,0:T(8,128)(2,1)S(1)}, u32[]{:S(2)}, u32[]{:S(2)}) collective-permute-start(bf16[5,128,128]{2,1,0:T(8,128)(2,1)S(1)} %add_convert_fusion.own_ref), channel_id=1, source_target_pairs={{0,16},{2,18},{4,20},{6,22},{8,24},{10,26},{12,28},{14,30},{16,0},... | collective-permute-start | bytes 491528 | tf_op jit(solution)/shard_map/ppermute | solution.py:291
  26.7 1.4 %own_coefficients.1 = (bf16[10,36,128,128]{3,2,1,0:T(8,128)(2,1)S(1)}, f32[8,128]{1,0:T(8,128)S(1)}) custom-call(s32[10,36]{1,0:T(8,128)S(1)} %copy-done.1, s32[10]{0:T(128)S(1)} %bitcast.12, f32[80,128]{1,0:T(8,128)S(1)} %convert_add_fusion.sums_ref, f32[80,128]{1,0:T(8,128)S(1)} %bitcast.8, ...), custom_call_target="tpu_custom_call", output_to_operand_aliasing={{0}: (4, {})} | custom-call | flops 754974720 | bytes 5898240 | tf_op jit(solution)/shard_map/own_coefficients/pallas_call | solution.py:370
  28.1 5.5 %collective-permute-done.7.crossed_ref = bf16[5,128,128]{2,1,0:T(8,128)(2,1)S(1)} collective-permute-done((bf16[5,128,128]{2,1,0:T(8,128)(2,1)S(1)}, bf16[5,128,128]{2,1,0:T(8,128)(2,1)S(1)}, u32[]{:S(2)}, u32[]{:S(2)}) %collective-permute-start.7) | collective-permute-done | bytes 163872 | tf_op jit(solution)/shard_map/ppermute | solution.py:291
  33.6 1.0 %collective-permute-start.11 = (bf16[5,128,128]{2,1,0:T(8,128)(2,1)S(1)}, bf16[5,128,128]{2,1,0:T(8,128)(2,1)S(1)}, u32[]{:S(2)}, u32[]{:S(2)}) collective-permute-start(bf16[5,128,128]{2,1,0:T(8,128)(2,1)S(1)} %get-tuple-element.22), channel_id=1, source_target_pairs={{0,1},{1,0},{2,3},{3,2},{4,5},{5,4},{6,7},{7,6},{8,9},{9,8},{10,11... | collective-permute-start | bytes 491528 | tf_op jit(solution)/shard_map/ppermute | solution.py:294
  34.7 0.0 collective-permute-start.10
  34.7 2.4 %collective-permute-start.9 = (bf16[5,128,128]{2,1,0:T(8,128)(2,1)S(1)}, bf16[5,128,128]{2,1,0:T(8,128)(2,1)S(1)}, u32[]{:S(2)}, u32[]{:S(2)}) collective-permute-start(bf16[5,128,128]{2,1,0:T(8,128)(2,1)S(1)} %get-tuple-element.21.refs_0_), channel_id=1, source_target_pairs={{0,8},{2,10},{4,12},{6,14},{8,0},{10,2},{12,4},{14,6},{16,24},{18,... | collective-permute-start | bytes 491528 | tf_op jit(solution)/shard_map/ppermute | solution.py:291
  37.1 1.1 %collective-permute-start.8 = (bf16[5,128,128]{2,1,0:T(8,128)(2,1)S(1)}, bf16[5,128,128]{2,1,0:T(8,128)(2,1)S(1)}, u32[]{:S(2)}, u32[]{:S(2)}) collective-permute-start(bf16[5,128,128]{2,1,0:T(8,128)(2,1)S(1)} %get-tuple-element.21.refs_0_), channel_id=1, source_target_pairs={{0,4},{2,6},{4,0},{6,2},{8,12},{10,14},{12,8},{14,10},{16,20},{18,... | collective-permute-start | bytes 491528 | tf_op jit(solution)/shard_map/ppermute | solution.py:291
  38.2 0.9 %collective-permute-done.11.refs_0_ = bf16[5,128,128]{2,1,0:T(8,128)(2,1)S(1)} collective-permute-done((bf16[5,128,128]{2,1,0:T(8,128)(2,1)S(1)}, bf16[5,128,128]{2,1,0:T(8,128)(2,1)S(1)}, u32[]{:S(2)}, u32[]{:S(2)}) %collective-permute-start.11) | collective-permute-done | bytes 163872 | tf_op jit(solution)/shard_map/ppermute | solution.py:294
  39.1 0.0 collective-permute-start.14
  39.1 1.8 %collective-permute-start.13 = (bf16[5,128,128]{2,1,0:T(8,128)(2,1)S(1)}, bf16[5,128,128]{2,1,0:T(8,128)(2,1)S(1)}, u32[]{:S(2)}, u32[]{:S(2)}) collective-permute-start(bf16[5,128,128]{2,1,0:T(8,128)(2,1)S(1)} %collective-permute-done.11.refs_0_), channel_id=1, source_target_pairs={{0,8},{2,10},{4,12},{6,14},{8,0},{10,2},{12,4},{14,6},{16,24},{18,... | collective-permute-start | bytes 491528 | tf_op jit(solution)/shard_map/ppermute | solution.py:291
  40.9 1.9 %collective-permute-done.10.refs_3_ = bf16[5,128,128]{2,1,0:T(8,128)(2,1)S(1)} collective-permute-done((bf16[5,128,128]{2,1,0:T(8,128)(2,1)S(1)}, bf16[5,128,128]{2,1,0:T(8,128)(2,1)S(1)}, u32[]{:S(2)}, u32[]{:S(2)}) %collective-permute-start.10) | collective-permute-done | bytes 163872 | tf_op jit(solution)/shard_map/ppermute | solution.py:291
  42.8 0.9 %collective-permute-start.12 = (bf16[5,128,128]{2,1,0:T(8,128)(2,1)S(1)}, bf16[5,128,128]{2,1,0:T(8,128)(2,1)S(1)}, u32[]{:S(2)}, u32[]{:S(2)}) collective-permute-start(bf16[5,128,128]{2,1,0:T(8,128)(2,1)S(1)} %collective-permute-done.11.refs_0_), channel_id=1, source_target_pairs={{0,4},{2,6},{4,0},{6,2},{8,12},{10,14},{12,8},{14,10},{16,20},{18,... | collective-permute-start | bytes 491528 | tf_op jit(solution)/shard_map/ppermute | solution.py:291
  43.7 2.0 %collective-permute-done.9.refs_2_ = bf16[5,128,128]{2,1,0:T(8,128)(2,1)S(1)} collective-permute-done((bf16[5,128,128]{2,1,0:T(8,128)(2,1)S(1)}, bf16[5,128,128]{2,1,0:T(8,128)(2,1)S(1)}, u32[]{:S(2)}, u32[]{:S(2)}) %collective-permute-start.9) | collective-permute-done | bytes 163872 | tf_op jit(solution)/shard_map/ppermute | solution.py:291
  45.7 2.0 %collective-permute-done.8.refs_1_ = bf16[5,128,128]{2,1,0:T(8,128)(2,1)S(1)} collective-permute-done((bf16[5,128,128]{2,1,0:T(8,128)(2,1)S(1)}, bf16[5,128,128]{2,1,0:T(8,128)(2,1)S(1)}, u32[]{:S(2)}, u32[]{:S(2)}) %collective-permute-start.8) | collective-permute-done | bytes 163872 | tf_op jit(solution)/shard_map/ppermute | solution.py:291
  47.8 0.1 collective-permute-start.15
  47.8 1.2 %collective-permute-done.14.refs_3_ = bf16[5,128,128]{2,1,0:T(8,128)(2,1)S(1)} collective-permute-done((bf16[5,128,128]{2,1,0:T(8,128)(2,1)S(1)}, bf16[5,128,128]{2,1,0:T(8,128)(2,1)S(1)}, u32[]{:S(2)}, u32[]{:S(2)}) %collective-permute-start.14) | collective-permute-done | bytes 163872 | tf_op jit(solution)/shard_map/ppermute | solution.py:291
  49.0 0.9 %collective-permute-done.13.refs_2_ = bf16[5,128,128]{2,1,0:T(8,128)(2,1)S(1)} collective-permute-done((bf16[5,128,128]{2,1,0:T(8,128)(2,1)S(1)}, bf16[5,128,128]{2,1,0:T(8,128)(2,1)S(1)}, u32[]{:S(2)}, u32[]{:S(2)}) %collective-permute-start.13) | collective-permute-done | bytes 163872 | tf_op jit(solution)/shard_map/ppermute | solution.py:291
  49.9 0.7 %collective-permute-done.12.refs_1_ = bf16[5,128,128]{2,1,0:T(8,128)(2,1)S(1)} collective-permute-done((bf16[5,128,128]{2,1,0:T(8,128)(2,1)S(1)}, bf16[5,128,128]{2,1,0:T(8,128)(2,1)S(1)}, u32[]{:S(2)}, u32[]{:S(2)}) %collective-permute-start.12) | collective-permute-done | bytes 163872 | tf_op jit(solution)/shard_map/ppermute | solution.py:291
  50.7 0.1 collective-permute-start.16
  50.8 0.0 collective-permute-done.15.home_core_ref
  50.8 0.1 own_collected.1.rest_0_
  50.9 1.9 %collective-permute-done.16.rest_1_ = bf16[20,128,128]{2,1,0:T(8,128)(2,1)S(1)} collective-permute-done((bf16[20,128,128]{2,1,0:T(8,128)(2,1)S(1)}, bf16[20,128,128]{2,1,0:T(8,128)(2,1)S(1)}, u32[]{:S(2)}, u32[]{:S(2)}) %collective-permute-start.16) | collective-permute-done | bytes 655392 | tf_op jit(solution)/shard_map/ppermute | solution.py:291
  52.8 1.9 %second_layer.2 = (bf16[5,128,128]{2,1,0:T(8,128)(2,1)S(1)}, bf16[80,128,128]{2,1,0:T(8,128)(2,1)S(1)}) custom-call(s32[10,36]{1,0:T(8,128)S(1)} %copy-done.1, s32[10]{0:T(128)S(1)} %bitcast.13, bf16[10,36,128,128]{3,2,1,0:T(8,128)(2,1)S(1)} %get-tuple-element.18.coef_ref, ...), custom_call_target="tpu_custom_call", output_to_operand_aliasing={{1}: (4, {})} | custom-call | flops 754974720 | bytes 5898240 | tf_op jit(solution)/shard_map/second_layer/pallas_call | solution.py:346
  54.7 1.7 %collective-permute-start.18 = (bf16[5,128,128]{2,1,0:T(8,128)(2,1)S(1)}, bf16[5,128,128]{2,1,0:T(8,128)(2,1)S(1)}, u32[]{:S(2)}, u32[]{:S(2)}) collective-permute-start(bf16[5,128,128]{2,1,0:T(8,128)(2,1)S(1)} %get-tuple-element.24.mine_ref), channel_id=1, source_target_pairs={{0,1},{1,0},{2,3},{3,2},{4,5},{5,4},{6,7},{7,6},{8,9},{9,8},{10,11... | collective-permute-start | bytes 491528 | tf_op jit(solution)/shard_map/ppermute | solution.py:294
  56.4 1.8 %second_layer.3.mine_ref = bf16[5,128,128]{2,1,0:T(8,128)(2,1)S(1)} custom-call(s32[10,36]{1,0:T(8,128)S(1)} %copy-done.1, s32[10]{0:T(128)S(1)} %bitcast.14, bf16[10,36,128,128]{3,2,1,0:T(8,128)(2,1)S(1)} %get-tuple-element.18.coef_ref, bf16[5,128,128]{2,1,0:T(8,128)(2,1)S(1)} %add_convert_fusion.own_ref, bf16[80,128,128]{2,1,0:T(8,128)(2,1)S(1)} %get-tuple-element.23.rest_0_), custom_call_target="tpu_custom_call" | custom-call | flops 754974720 | bytes 5898240 | tf_op jit(solution)/shard_map/second_layer/pallas_call | solution.py:346
  58.3 0.4 collective-permute-start.17
  58.7 2.5 %collective-permute-done.18.other_ref = bf16[5,128,128]{2,1,0:T(8,128)(2,1)S(1)} collective-permute-done((bf16[5,128,128]{2,1,0:T(8,128)(2,1)S(1)}, bf16[5,128,128]{2,1,0:T(8,128)(2,1)S(1)}, u32[]{:S(2)}, u32[]{:S(2)}) %collective-permute-start.18) | collective-permute-done | bytes 163872 | tf_op jit(solution)/shard_map/ppermute | solution.py:294
  61.2 0.7 %result.2.rest_0_ = bf16[10,128,128]{2,1,0:T(8,128)(2,1)} custom-call(bf16[5,128,128]{2,1,0:T(8,128)(2,1)S(1)} %get-tuple-element.24.mine_ref, bf16[5,128,128]{2,1,0:T(8,128)(2,1)S(1)} %collective-permute-done.18.other_ref), custom_call_target="tpu_custom_call" | custom-call | tf_op jit(solution)/shard_map/result/pallas_call | solution.py:424
  61.9 2.2 %collective-permute-done.17.other_ref = bf16[5,128,128]{2,1,0:T(8,128)(2,1)S(1)} collective-permute-done((bf16[5,128,128]{2,1,0:T(8,128)(2,1)S(1)}, bf16[5,128,128]{2,1,0:T(8,128)(2,1)S(1)}, u32[]{:S(2)}, u32[]{:S(2)}) %collective-permute-start.17) | collective-permute-done | bytes 163872 | tf_op jit(solution)/shard_map/ppermute | solution.py:294
  64.2 0.7 %result.3 = bf16[10,128,128]{2,1,0:T(8,128)(2,1)} custom-call(bf16[5,128,128]{2,1,0:T(8,128)(2,1)S(1)} %second_layer.3.mine_ref, bf16[5,128,128]{2,1,0:T(8,128)(2,1)S(1)} %collective-permute-done.17.other_ref, bf16[10,128,128]{2,1,0:T(8,128)(2,1)} %result.2.rest_0_), custom_call_target="tpu_custom_call", output_to_operand_aliasing={{}: (2, {})} | custom-call | tf_op jit(solution)/shard_map/result/pallas_call | solution.py:424
  (7 shorter events, 0.2 us)
Async XLA Ops:
  0.0 17.8 %copy-start.1 = (s32[10,36]{1,0:T(8,128)S(1)}, s32[10,36]{1,0:T(8,128)}, u32[]{:S(2)}) copy-start(s32[10,36]{1,0:T(8,128)} %cols_ref.9) | copy-start | bytes 4324
  0.0 17.8 %copy-start.2 = (s32[10,1]{0,1:T(1,128)S(1)}, s32[10,1]{0,1:T(1,128)}, u32[]{:S(2)}) copy-start(s32[10,1]{0,1:T(1,128)} %param.7) | copy-start | bytes 124
  0.0 17.8 %copy-start = (f32[10240]{0:T(1024)S(1)}, f32[10240]{0:T(1024)}, u32[]{:S(2)}) copy-start(f32[10240]{0:T(1024)} %param.9) | copy-start | bytes 122884
  3.3 4.8 %collective-permute-start.1 = (bf16[80,128]{1,0:T(8,128)(2,1)S(1)}, bf16[80,128]{1,0:T(8,128)(2,1)S(1)}, u32[]{:S(2)}, u32[]{:S(2)}) collective-permute-start(bf16[80,128]{1,0:T(8,128)(2,1)S(1)} %convert_element_type.36), channel_id=1, source_target_pairs={{0,4},{2,6},{4,0},{6,2},{8,12},{10,14},{12,8},{14,10},{16,20},{18,... | collective-permute-start | bytes 61448 | tf_op jit(solution)/shard_map/ppermute | solution.py:291
  6.3 1.8 %collective-permute-start = (bf16[80,128]{1,0:T(8,128)(2,1)S(1)}, bf16[80,128]{1,0:T(8,128)(2,1)S(1)}, u32[]{:S(2)}, u32[]{:S(2)}) collective-permute-start(bf16[80,128]{1,0:T(8,128)(2,1)S(1)} %convert_element_type.36), channel_id=1, source_target_pairs={{0,2},{2,0},{4,6},{6,4},{8,10},{10,8},{12,14},{14,12},{16,18},{18,... | collective-permute-start | bytes 61448 | tf_op jit(solution)/shard_map/ppermute | solution.py:291
  6.3 3.2 %collective-permute-start.2 = (bf16[80,128]{1,0:T(8,128)(2,1)S(1)}, bf16[80,128]{1,0:T(8,128)(2,1)S(1)}, u32[]{:S(2)}, u32[]{:S(2)}) collective-permute-start(bf16[80,128]{1,0:T(8,128)(2,1)S(1)} %convert_element_type.36), channel_id=1, source_target_pairs={{0,6},{2,4},{4,2},{6,0},{8,14},{10,12},{12,10},{14,8},{16,22},{18,... | collective-permute-start | bytes 61448 | tf_op jit(solution)/shard_map/ppermute | solution.py:291
  9.6 6.0 %collective-permute-start.5 = (bf16[80,128]{1,0:T(8,128)(2,1)S(1)}, bf16[80,128]{1,0:T(8,128)(2,1)S(1)}, u32[]{:S(2)}, u32[]{:S(2)}) collective-permute-start(bf16[80,128]{1,0:T(8,128)(2,1)S(1)} %add_convert_fusion.1._), channel_id=1, source_target_pairs={{0,16},{2,18},{4,20},{6,22},{8,24},{10,26},{12,28},{14,30},{16,0},... | collective-permute-start | bytes 61448 | tf_op jit(solution)/shard_map/ppermute | solution.py:291
  12.2 5.6 %collective-permute-start.4 = (bf16[80,128]{1,0:T(8,128)(2,1)S(1)}, bf16[80,128]{1,0:T(8,128)(2,1)S(1)}, u32[]{:S(2)}, u32[]{:S(2)}) collective-permute-start(bf16[80,128]{1,0:T(8,128)(2,1)S(1)} %add_convert_fusion.1._), channel_id=1, source_target_pairs={{0,24},{2,26},{4,28},{6,30},{8,16},{10,18},{12,20},{14,22},{16,8},... | collective-permute-start | bytes 61448 | tf_op jit(solution)/shard_map/ppermute | solution.py:291
  13.8 4.0 %collective-permute-start.3 = (bf16[80,128]{1,0:T(8,128)(2,1)S(1)}, bf16[80,128]{1,0:T(8,128)(2,1)S(1)}, u32[]{:S(2)}, u32[]{:S(2)}) collective-permute-start(bf16[80,128]{1,0:T(8,128)(2,1)S(1)} %add_convert_fusion.1._), channel_id=1, source_target_pairs={{0,8},{2,10},{4,12},{6,14},{8,0},{10,2},{12,4},{14,6},{16,24},{18,... | collective-permute-start | bytes 61448 | tf_op jit(solution)/shard_map/ppermute | solution.py:291
  19.7 5.4 %collective-permute-start.6 = (bf16[5,128,128]{2,1,0:T(8,128)(2,1)S(1)}, bf16[5,128,128]{2,1,0:T(8,128)(2,1)S(1)}, u32[]{:S(2)}, u32[]{:S(2)}) collective-permute-start(bf16[5,128,128]{2,1,0:T(8,128)(2,1)S(1)} %first_layer.2.rest_0_), channel_id=1, source_target_pairs={{0,1},{1,0},{2,3},{3,2},{4,5},{5,4},{6,7},{7,6},{8,9},{9,8},{10,11... | collective-permute-start | bytes 491528 | tf_op jit(solution)/shard_map/ppermute | solution.py:294
  25.1 8.5 %collective-permute-start.7 = (bf16[5,128,128]{2,1,0:T(8,128)(2,1)S(1)}, bf16[5,128,128]{2,1,0:T(8,128)(2,1)S(1)}, u32[]{:S(2)}, u32[]{:S(2)}) collective-permute-start(bf16[5,128,128]{2,1,0:T(8,128)(2,1)S(1)} %add_convert_fusion.own_ref), channel_id=1, source_target_pairs={{0,16},{2,18},{4,20},{6,22},{8,24},{10,26},{12,28},{14,30},{16,0},... | collective-permute-start | bytes 491528 | tf_op jit(solution)/shard_map/ppermute | solution.py:291
  33.6 5.5 %collective-permute-start.11 = (bf16[5,128,128]{2,1,0:T(8,128)(2,1)S(1)}, bf16[5,128,128]{2,1,0:T(8,128)(2,1)S(1)}, u32[]{:S(2)}, u32[]{:S(2)}) collective-permute-start(bf16[5,128,128]{2,1,0:T(8,128)(2,1)S(1)} %get-tuple-element.22), channel_id=1, source_target_pairs={{0,1},{1,0},{2,3},{3,2},{4,5},{5,4},{6,7},{7,6},{8,9},{9,8},{10,11... | collective-permute-start | bytes 491528 | tf_op jit(solution)/shard_map/ppermute | solution.py:294
  34.7 8.1 %collective-permute-start.10 = (bf16[5,128,128]{2,1,0:T(8,128)(2,1)S(1)}, bf16[5,128,128]{2,1,0:T(8,128)(2,1)S(1)}, u32[]{:S(2)}, u32[]{:S(2)}) collective-permute-start(bf16[5,128,128]{2,1,0:T(8,128)(2,1)S(1)} %get-tuple-element.21.refs_0_), channel_id=1, source_target_pairs={{0,12},{2,14},{4,8},{6,10},{8,4},{10,6},{12,0},{14,2},{16,28},{18,... | collective-permute-start | bytes 491528 | tf_op jit(solution)/shard_map/ppermute | solution.py:291
  34.7 11.0 %collective-permute-start.9 = (bf16[5,128,128]{2,1,0:T(8,128)(2,1)S(1)}, bf16[5,128,128]{2,1,0:T(8,128)(2,1)S(1)}, u32[]{:S(2)}, u32[]{:S(2)}) collective-permute-start(bf16[5,128,128]{2,1,0:T(8,128)(2,1)S(1)} %get-tuple-element.21.refs_0_), channel_id=1, source_target_pairs={{0,8},{2,10},{4,12},{6,14},{8,0},{10,2},{12,4},{14,6},{16,24},{18,... | collective-permute-start | bytes 491528 | tf_op jit(solution)/shard_map/ppermute | solution.py:291
  37.1 10.7 %collective-permute-start.8 = (bf16[5,128,128]{2,1,0:T(8,128)(2,1)S(1)}, bf16[5,128,128]{2,1,0:T(8,128)(2,1)S(1)}, u32[]{:S(2)}, u32[]{:S(2)}) collective-permute-start(bf16[5,128,128]{2,1,0:T(8,128)(2,1)S(1)} %get-tuple-element.21.refs_0_), channel_id=1, source_target_pairs={{0,4},{2,6},{4,0},{6,2},{8,12},{10,14},{12,8},{14,10},{16,20},{18,... | collective-permute-start | bytes 491528 | tf_op jit(solution)/shard_map/ppermute | solution.py:291
  39.1 9.9 %collective-permute-start.14 = (bf16[5,128,128]{2,1,0:T(8,128)(2,1)S(1)}, bf16[5,128,128]{2,1,0:T(8,128)(2,1)S(1)}, u32[]{:S(2)}, u32[]{:S(2)}) collective-permute-start(bf16[5,128,128]{2,1,0:T(8,128)(2,1)S(1)} %collective-permute-done.11.refs_0_), channel_id=1, source_target_pairs={{0,12},{2,14},{4,8},{6,10},{8,4},{10,6},{12,0},{14,2},{16,28},{18,... | collective-permute-start | bytes 491528 | tf_op jit(solution)/shard_map/ppermute | solution.py:291
  39.1 10.8 %collective-permute-start.13 = (bf16[5,128,128]{2,1,0:T(8,128)(2,1)S(1)}, bf16[5,128,128]{2,1,0:T(8,128)(2,1)S(1)}, u32[]{:S(2)}, u32[]{:S(2)}) collective-permute-start(bf16[5,128,128]{2,1,0:T(8,128)(2,1)S(1)} %collective-permute-done.11.refs_0_), channel_id=1, source_target_pairs={{0,8},{2,10},{4,12},{6,14},{8,0},{10,2},{12,4},{14,6},{16,24},{18,... | collective-permute-start | bytes 491528 | tf_op jit(solution)/shard_map/ppermute | solution.py:291
  42.8 7.8 %collective-permute-start.12 = (bf16[5,128,128]{2,1,0:T(8,128)(2,1)S(1)}, bf16[5,128,128]{2,1,0:T(8,128)(2,1)S(1)}, u32[]{:S(2)}, u32[]{:S(2)}) collective-permute-start(bf16[5,128,128]{2,1,0:T(8,128)(2,1)S(1)} %collective-permute-done.11.refs_0_), channel_id=1, source_target_pairs={{0,4},{2,6},{4,0},{6,2},{8,12},{10,14},{12,8},{14,10},{16,20},{18,... | collective-permute-start | bytes 491528 | tf_op jit(solution)/shard_map/ppermute | solution.py:291
  47.8 3.0 %collective-permute-start.15 = (bf16[20,128,128]{2,1,0:T(8,128)(2,1)S(1)}, bf16[20,128,128]{2,1,0:T(8,128)(2,1)S(1)}, u32[]{:S(2)}, u32[]{:S(2)}) collective-permute-start(bf16[20,128,128]{2,1,0:T(8,128)(2,1)S(1)} %own_joined.2.home_ref), channel_id=1, source_target_pairs={{0,2},{2,0},{4,6},{6,4},{8,10},{10,8},{12,14},{14,12},{16,18},{18,... | collective-permute-start | bytes 1966088 | tf_op jit(solution)/shard_map/ppermute | solution.py:291
  50.7 2.2 %collective-permute-start.16 = (bf16[20,128,128]{2,1,0:T(8,128)(2,1)S(1)}, bf16[20,128,128]{2,1,0:T(8,128)(2,1)S(1)}, u32[]{:S(2)}, u32[]{:S(2)}) collective-permute-start(bf16[20,128,128]{2,1,0:T(8,128)(2,1)S(1)} %own_joined.3.away_ref), channel_id=1, source_target_pairs={{0,2},{2,0},{4,6},{6,4},{8,10},{10,8},{12,14},{14,12},{16,18},{18,... | collective-permute-start | bytes 1966088 | tf_op jit(solution)/shard_map/ppermute | solution.py:291
  54.7 6.5 %collective-permute-start.18 = (bf16[5,128,128]{2,1,0:T(8,128)(2,1)S(1)}, bf16[5,128,128]{2,1,0:T(8,128)(2,1)S(1)}, u32[]{:S(2)}, u32[]{:S(2)}) collective-permute-start(bf16[5,128,128]{2,1,0:T(8,128)(2,1)S(1)} %get-tuple-element.24.mine_ref), channel_id=1, source_target_pairs={{0,1},{1,0},{2,3},{3,2},{4,5},{5,4},{6,7},{7,6},{8,9},{9,8},{10,11... | collective-permute-start | bytes 491528 | tf_op jit(solution)/shard_map/ppermute | solution.py:294
  58.3 5.9 %collective-permute-start.17 = (bf16[5,128,128]{2,1,0:T(8,128)(2,1)S(1)}, bf16[5,128,128]{2,1,0:T(8,128)(2,1)S(1)}, u32[]{:S(2)}, u32[]{:S(2)}) collective-permute-start(bf16[5,128,128]{2,1,0:T(8,128)(2,1)S(1)} %second_layer.3.mine_ref), channel_id=1, source_target_pairs={{0,1},{1,0},{2,3},{3,2},{4,5},{5,4},{6,7},{7,6},{8,9},{9,8},{10,11... | collective-permute-start | bytes 491528 | tf_op jit(solution)/shard_map/ppermute | solution.py:294
